TPU v7x, 32 devices: a whole 2x2x4 slice. The times are simulated.
32 devices in a mesh: groups: 2 (over y), replica: 4 (over z), tensor: 4 (over x, core).
Axes of the slice: x: 2, y: 2, z: 4, core: 2. Of those that a mesh axis runs over, the one named last changes fastest.
Arguments:
- queries: bfloat16 [1024, 2, 4096], P(('groups', 'replica'), None, 'tensor'), parts along dimension 0, may hold values from -8 to 8
- recent_keys: bfloat16 [1024, 2, 1024], P(('groups', 'replica'), None, 'tensor'), parts along dimension 0, may hold values from -12 to 12
- recent_values: bfloat16 [1024, 2, 1024], P(('groups', 'replica'), None, 'tensor'), parts along dimension 0, may hold values from -24 to 24
- prefix_key_value: bfloat16 [8, 2, 4096, 1024], P(('groups', 'replica'), None, None, 'tensor'), parts along dimension 0, may hold values from -6 to 6
- prefix_length_each: int32 [1024], P(('groups', 'replica')), parts along dimension 0, may hold values from 512 to 4096, as said below
- batch_adapter_index: int32 [128], P(('groups', 'replica')), parts along dimension 0, may hold values from 0 to 63, as said below
- adapter_table_row: int32 [128], P('groups'), parts along dimension 0, may hold values from 0 to 63, as said below
- down_weight_table: bfloat16 [64, 16, 4096], P('replica', None, 'tensor'), may hold values from -2 to 2
- up_weight_table: bfloat16 [64, 16, 8192], P('replica', None, 'tensor'), may hold values from -1.5 to 1.5
- output_weight: bfloat16 [4096, 8192], P('tensor'), may hold values from -2 to 2
Outputs:
- block_out: bfloat16 [1024, 2, 8192], P(('groups', 'replica'), None, 'tensor'), parts along dimension 0
There are 2 independent parts, one for each index of `groups`. A program takes and returns all parts, laid end to end along the dimension named above; an argument that names none is the same for every part. Nothing has to cross between parts.
Inputs may be any that keep to these rules, and one draw needn't show every extreme that they name: `prefix_length_each`: the largest length equals 4096 in every draw. adapter_table_row is a permutation of 0 to 63; rows k * 16 to (k + 1) * 16 - 1 of the tables lie on replica k. `batch_adapter_index`: of the 16 fork batches of one replica, at most 8 name adapters whose table rows lie on one replica; every draw reaches 8. An adapter may serve several batches.
All inputs are finite; a program needn't handle non-finite values.
Results may differ from a plain program's by a relative error of at most 0.0095.
Values may be sent and summed in bfloat16 or wider, within the bound.
No kernel may reach another device: no remote copies, remote signals or barrier semaphores. Data moves between devices by JAX's collectives and lax.ppermute only.
A program may use at most 192 MiB of HBM per device.

v0:
```python
import math

import jax
import jax.numpy as jnp
from jax import lax
from jax.sharding import PartitionSpec as P

HD = 128


def lookup(wanted, adapter_table_row):
    table_size = adapter_table_row.shape[0]
    matches = wanted[..., None] == jnp.arange(table_size, dtype=jnp.int32)
    return jnp.sum(jnp.where(matches, adapter_table_row, 0), axis=-1)


def body(
    queries,
    recent_keys,
    recent_values,
    prefix_key_value,
    prefix_length_each,
    batch_adapter_index,
    adapter_table_row,
    down_weight_table,
    up_weight_table,
    output_weight,
):
    forks_total, steps_total, query_width = queries.shape
    heads_kv = recent_keys.shape[2] // HD
    group_size = query_width // (heads_kv * HD)
    prefix_len = prefix_key_value.shape[2]
    score_scale = 1.0 / math.sqrt(HD)
    query_heads = queries.reshape(forks_total, steps_total, heads_kv, group_size, HD)
    key_rows = prefix_key_value[0, 0].reshape(prefix_len, heads_kv, HD)
    value_rows = prefix_key_value[0, 1].reshape(prefix_len, heads_kv, HD)
    new_key = recent_keys.reshape(forks_total, steps_total, heads_kv, HD)
    new_value = recent_values.reshape(forks_total, steps_total, heads_kv, HD)
    causal = jnp.arange(steps_total)[None, :] <= jnp.arange(steps_total)[:, None]
    own_scores = (
        jnp.einsum("fsvgd,ftvd->vfsgt", query_heads, new_key, preferred_element_type=jnp.float32)
        * score_scale
    )
    own_scores = jnp.where(causal[None, None, :, None, :], own_scores, -jnp.inf)
    scores = (
        jnp.einsum("fsvgd,pvd->vfsgp", query_heads, key_rows, preferred_element_type=jnp.float32)
        * score_scale
    )
    visible = jnp.arange(prefix_len, dtype=jnp.int32)[None, :] < prefix_length_each[:, None]
    scores = jnp.where(visible[None, :, None, None, :], scores, -jnp.inf)
    top_score = jnp.maximum(jnp.max(scores, axis=-1), jnp.max(own_scores, axis=-1))
    weights = jnp.exp(scores - top_score[..., None])
    own_weights = jnp.exp(own_scores - top_score[..., None])
    totals = jnp.sum(weights, axis=-1) + jnp.sum(own_weights, axis=-1)
    mixture = jnp.einsum(
        "vfsgp,pvd->vfsgd",
        weights.astype(jnp.bfloat16),
        value_rows,
        preferred_element_type=jnp.float32,
    )
    mixture = mixture + jnp.einsum(
        "vfsgt,ftvd->vfsgd",
        own_weights.astype(jnp.bfloat16),
        new_value,
        preferred_element_type=jnp.float32,
    )
    attended = mixture / totals[..., None]
    attended = (
        attended.transpose(1, 2, 0, 3, 4)
        .reshape(forks_total, steps_total, query_width)
        .astype(jnp.bfloat16)
    )
    flat_rows = attended.reshape(forks_total * steps_total, query_width)
    partial_value = jnp.dot(flat_rows, output_weight, preferred_element_type=jnp.float32)
    base_output = lax.psum_scatter(
        partial_value.astype(jnp.bfloat16), "tensor", scatter_dimension=1, tiled=True
    ).astype(jnp.float32)
    batch_groups = batch_adapter_index.shape[0]
    rank_width = down_weight_table.shape[1]
    output_width = up_weight_table.shape[2]
    split_at = rank_width * query_width
    own_rows = lookup(batch_adapter_index, adapter_table_row)
    whole_a, whole_b = (
        lax.all_gather(down_weight_table, "replica", axis=0, tiled=True),
        lax.all_gather(up_weight_table, "replica", axis=0, tiled=True),
    )
    total_adapters = whole_a.shape[0]
    full_table = jnp.concatenate(
        [
            whole_a.reshape(total_adapters, split_at),
            whole_b.reshape(total_adapters, rank_width * output_width),
        ],
        axis=1,
    )
    picker = (own_rows[:, None] == jnp.arange(total_adapters, dtype=jnp.int32)[None, :]).astype(
        jnp.bfloat16
    )
    slot_data = jnp.dot(picker, full_table, preferred_element_type=jnp.float32).astype(jnp.bfloat16)
    a_slots = slot_data[:, :split_at].reshape(batch_groups, rank_width, query_width)
    up_slots = slot_data[:, split_at:].reshape(batch_groups, rank_width, output_width)
    grouped = attended.reshape(batch_groups, forks_total * steps_total // batch_groups, query_width)
    rank_activation = jnp.einsum(
        "brq,bkq->brk", grouped, a_slots, preferred_element_type=jnp.float32
    )
    rank_activation = lax.psum(rank_activation, "tensor")
    adapter_output = jnp.einsum(
        "yzh,yhf->yzf",
        rank_activation,
        up_slots.astype(jnp.float32),
        precision=lax.Precision.HIGHEST,
    )
    final_output = (
        base_output.reshape(batch_groups, forks_total * steps_total // batch_groups, output_width)
        + adapter_output
    )
    return final_output.reshape(forks_total, steps_total, output_width).astype(jnp.bfloat16)


def solution(mesh):
    placed = (
        P(("groups", "replica"), None, "tensor"),
        P(("groups", "replica"), None, "tensor"),
        P(("groups", "replica"), None, "tensor"),
        P(("groups", "replica"), None, None, "tensor"),
        P(("groups", "replica")),
        P(("groups", "replica")),
        P("groups"),
        P("replica", None, "tensor"),
        P("replica", None, "tensor"),
        P("tensor", None),
    )
    return jax.shard_map(
        body,
        mesh=mesh,
        in_specs=placed,
        out_specs=P(("groups", "replica"), None, "tensor"),
        check_vma=False,
    )
```

profile of v0, /device:TPU:0, one launch (start us, length us, event | category | flops | bytes accessed | tf_op | source)
XLA Modules:
  0.0 172.3 jit_solution(18352775149607593984)
XLA Ops:
  7.4 0.0 all-gather.3.cloned.1.call-start
  7.4 0.7 all-gather.3.cloned.1.call-update
  8.1 0.0 all-gather.5.cloned.1.call-start
  8.1 0.7 all-gather.5.cloned.1.call-update
  8.8 0.0 reduce-scatter.2.cloned.1.call-start
  8.9 0.0 copy-start.1
  8.9 0.0 copy-start.2
  8.9 3.9 %fusion.36 = (bf16[1,1,4096,256]{3,2,1,0:T(8,128)(2,1)S(1)}, bf16[1,1,4096,256]{3,2,1,0:T(8,128)(2,1)}) fusion(bf16[1,2,4096,256]{3,2,1,0:T(8,128)(2,1)} %param.13), kind=kLoop, calls=%fused_computation.39 | loop fusion | bytes 8388608 | tf_op jit(solution)/shard_map/slice | solution.py:35
  12.8 4.1 %copy.83 = bf16[1,1,4096,256]{2,3,1,0:T(8,128)(2,1)} copy(bf16[1,1,4096,256]{3,2,1,0:T(8,128)(2,1)} %get-tuple-element.6) | data formatting | bytes 4194304
  16.9 0.0 copy-done.4
  17.0 0.4 iota_compare_fusion
  17.3 2.9 %copy.82 = bf16[1,1,4096,256]{2,3,1,0:T(8,128)(2,1)} copy(bf16[1,1,4096,256]{3,2,1,0:T(8,128)(2,1)S(1)} %get-tuple-element.5) | data formatting | bytes 4194304
  20.2 0.0 copy-done.1
  20.2 0.3 reshape.78
  20.6 0.0 copy-done.2
  20.6 0.1 reshape.79
  20.7 4.7 %fusion.37 = (f32[2,128,2,4]{3,2,1,0:T(2,128)S(1)}, f32[2,128,2,4,2]{3,4,2,1,0:T(2,128)S(1)}) fusion(bf16[128,2,2,128,1]{3,2,1,0,4:T(2,128)(2,1)S(1)} %bitcast.50, bf16[128,2,2,4,128]{4,3,2,1,0:T(4,128)(2,1)S(1)} %reshape.78, pred[2,2]{1,0:T(4,128)(4,1)S(1)} %iota_compare_fusion.4), kind=kOutput, calls=%fused_computation.40 | convolution fusion | flops 1058816 | bytes 679940 | tf_op jit(solution)/shard_map/fsvgd,ftvd->vfsgt/dot_general | solution.py:41
  25.4 0.1 copy.61
  25.5 15.6 %fusion = (f32[2,128,2,4]{1,3,2,0:T(4,128)S(1)}, f32[2,128,2,4,4096]{4,1,3,2,0:T(8,128)}) fusion(pred[128,4096]{1,0:T(8,128)(4,1)S(1)} %iota_compare_fusion, bf16[4096,2,128,1,1]{0,2,4,3,1:T(8,128)(2,1)} %bitcast.38, bf16[128,2,2,4,128]{4,3,2,1,0:T(4,128)(2,1)S(1)} %reshape.78), kind=kOutput, calls=%fused_computation.3 | convolution fusion | flops 2172647424 | bytes 36708352 | tf_op jit(solution)/shard_map/fsvgd,pvd->vfsgp/dot_general | solution.py:46
  41.2 0.2 copy.64
  41.3 0.1 reshape.80
  41.4 1.0 fusion.26
  42.5 0.1 copy.67
  42.6 15.2 %fusion.1 = f32[2,128,2,4]{1,3,2,0:T(4,128)S(1)} fusion(f32[2,128,2,4,4096]{4,1,3,2,0:T(8,128)} %get-tuple-element.8, f32[2,128,2,4]{1,3,2,0:T(4,128)S(1)} %max.7, pred[128,4096]{1,0:T(8,128)(4,1)S(1)} %iota_compare_fusion), kind=kLoop, calls=%fused_computation.4 | loop fusion | flops 33552384 | bytes 34095104 | tf_op jit(solution)/shard_map/reduce_sum | solution.py:54
  57.8 0.6 add_bitcast_fusion
  58.4 1.6 fusion.28
  60.0 15.9 %fusion.19 = bf16[128,2,2,4,128]{4,0,3,1,2:T(8,128)(2,1)S(1)} fusion(bf16[4096,2,128,1,1]{0,2,4,3,1:T(8,128)(2,1)S(1)} %bitcast.44, f32[2,128,2,4,4096]{4,1,3,2,0:T(8,128)} %get-tuple-element.8, f32[2,128,2,4]{1,3,2,0:T(4,128)S(1)} %max.7, pred[128,4096]{1,0:T(8,128)(4,1)S(1)} %iota_compare_fusion, f32[2,128,2,4,128]{4,3,2,1,0:T(4,128)} %fusion.28, ...), kind=kOutput, calls=%fused_computation.18 | convolution fusion | flops 2181824512 | bytes 37765120 | tf_op jit(solution)/shard_map/vfsgp,pvd->vfsgd/dot_general | solution.py:55
  75.9 0.4 copy.68
  76.3 0.4 convert_element_type.35
  76.7 0.0 copy-start.5
  76.7 0.0 copy-start.6
  76.7 11.9 %convolution_convert_fusion.1 = bf16[256,8192]{1,0:T(8,128)(2,1)} fusion(bf16[256,1024]{1,0:T(8,128)(2,1)S(1)} %convert_element_type.35, bf16[1024,8192]{1,0:T(8,128)(2,1)} %param.19), kind=kOutput, calls=%fused_computation.8 | convolution fusion | flops 4297064448 | bytes 21495808 | tf_op jit(solution)/shard_map/dot_general | solution.py:74
  88.6 0.0 reduce-scatter.2.cloned.1.call-update
  88.6 0.4 convert_element_type.37
  89.0 0.2 select_reduce_fusion
  89.2 0.0 all-gather.3.cloned.1.call-done
  89.2 2.9 %copy.84 = bf16[8,8,16,1024]{3,1,2,0:T(8,128)(2,1)S(1)} copy(bf16[8,8,16,1024]{3,2,1,0:T(8,128)(2,1)} %bitcast.43) | data formatting | bytes 4194304
  92.1 47.4 %all-gather.5.cloned.1.call-done = bf16[64,16,2048]{2,1,0:T(8,128)(2,1)} async-done(((bf16[16,16,2048]{2,1,0:T(8,128)(2,1)}), bf16[64,16,2048]{2,1,0:T(8,128)(2,1)}) %all-gather.5.cloned.1.call-update) | async-done | bytes 4194320 | tf_op jit(solution)/shard_map/all_gather | solution.py:85
  139.5 4.6 %copy.85 = bf16[8,8,16,2048]{3,1,2,0:T(8,128)(2,1)S(1)} copy(bf16[8,8,16,2048]{3,2,1,0:T(8,128)(2,1)} %bitcast.40) | data formatting | bytes 8388608
  144.1 2.7 %convolution_convert_fusion = bf16[16,49152]{1,0:T(8,128)(2,1)S(1)} fusion(bf16[64,32768]{1,0:T(8,128)(2,1)S(1)} %bitcast.41, bf16[64,16384]{1,0:T(8,128)(2,1)S(1)} %bitcast.45, s32[16]{0:T(128)S(1)} %select_reduce_fusion), kind=kOutput, calls=%fused_computation | convolution fusion | flops 114033664 | bytes 7864384 | tf_op jit(solution)/shard_map/dot_general | solution.py:98
  146.8 0.1 slice.17
  146.9 0.3 copy.86
  147.2 0.6 copy.87
  147.8 0.3 fusion.38
  148.1 13.0 %psum.7 = f32[16,16,16]{2,1,0:T(8,128)S(1)} all-reduce(f32[16,16,16]{2,1,0:T(8,128)S(1)} %fusion.38), channel_id=1, replica_groups=mesh['groups'=2,'replica'=4,'tensor'=4] {'tensor'}, use_global_device_ids=true, to_apply=%region_6.7 | all-reduce | flops 4096 | bytes 32768 | tf_op jit(solution)/shard_map/psum | solution.py:105
  161.1 0.0 reduce-scatter.2.cloned.1.call-done
  161.1 2.2 %fusion.9 = bf16[16,16,2048]{2,1,0:T(8,128)(2,1)S(1)} fusion(f32[16,16,16]{2,1,0:T(8,128)S(1)} %psum.7, bf16[16,16,2048]{2,1,0:T(8,128)(2,1)S(1)} %bitcast.39, bf16[16,16,2048]{2,1,0:T(8,128)(2,1)} %bitcast.48), kind=kOutput, calls=%fused_computation.13 | convolution fusion | flops 102236160 | bytes 3162112 | tf_op jit(solution)/shard_map/yzh,yhf->yzf/dot_general | solution.py:106
  163.4 1.5 convert_element_type.40
  (10 shorter events, 0.1 us)
Async XLA Ops:
  7.4 9.6 %copy-start.4 = (s32[128]{0:T(128)S(1)}, s32[128]{0:T(128)}, u32[]{:S(2)}) copy-start(s32[128]{0:T(128)} %param.14) | copy-start | bytes 1540
  7.4 81.8 %all-gather.3.cloned.1.call-start = ((), (), s32[]{:S(2)}) async-start(), calls=%async_computation.2 | async-start | bytes 2621440 | tf_op jit(solution)/shard_map/all_gather | solution.py:84
  8.1 131.4 %all-gather.5.cloned.1.call-start = ((), (), s32[]{:S(2)}) async-start(), calls=%async_computation.3 | async-start | bytes 5242880 | tf_op jit(solution)/shard_map/all_gather | solution.py:85
  8.8 152.3 %reduce-scatter.2.cloned.1.call-start = ((), (), s32[]{:S(2)}) async-start(), calls=%async_computation.1 | async-start | bytes 5242880 | tf_op jit(solution)/shard_map/reduce_scatter | solution.py:75
  8.9 11.3 %copy-start.1 = (bf16[128,2,1024]{2,1,0:T(2,128)(2,1)S(1)}, bf16[128,2,1024]{2,1,0:T(2,128)(2,1)}, u32[]{:S(2)}) copy-start(bf16[128,2,1024]{2,1,0:T(2,128)(2,1)} %param.10) | copy-start | bytes 1572868
  8.9 11.7 %copy-start.2 = (bf16[128,2,256]{2,1,0:T(2,128)(2,1)S(1)}, bf16[128,2,256]{2,1,0:T(2,128)(2,1)}, u32[]{:S(2)}) copy-start(bf16[128,2,256]{2,1,0:T(2,128)(2,1)} %param.11) | copy-start | bytes 393220
  25.5 15.8 %copy-start.3 = (bf16[128,2,256]{2,1,0:T(2,128)(2,1)S(1)}, bf16[128,2,256]{2,1,0:T(2,128)(2,1)}, u32[]{:S(2)}) copy-start(bf16[128,2,256]{2,1,0:T(2,128)(2,1)} %param.12) | copy-start | bytes 393220
  42.6 17.4 %copy-start = (bf16[1,1,4096,256]{2,3,1,0:T(8,128)(2,1)S(1)}, bf16[1,1,4096,256]{2,3,1,0:T(8,128)(2,1)}, u32[]{:S(2)}) copy-start(bf16[1,1,4096,256]{2,3,1,0:T(8,128)(2,1)} %copy.83) | copy-start | bytes 6291460
  76.7 12.3 %copy-start.5 = (s32[64]{0:T(128)S(1)}, s32[64]{0:T(128)}, u32[]{:S(2)}) copy-start(s32[64]{0:T(128)} %param.16) | copy-start | bytes 772
  76.7 12.3 %copy-start.6 = (s32[16]{0:T(128)S(1)}, s32[16]{0:T(128)}, u32[]{:S(2)}) copy-start(s32[16]{0:T(128)} %param.15) | copy-start | bytes 196
Sparse Core Ops, SparseCore 0:
  9.8 48.6 all-gather.2
  60.0 79.4 all-gather.4
Sparse Core Ops, SparseCore 1:
  88.7 47.1 reduce-scatter.1
where the time goes:
time: 173 us; the launch traced here: 172 us
  matrix products  55 us (32%)
  waiting for transfers between devices  48.9 us (28%)
  local copies, waits for them, and re-layouts  22.9 us (13%)
  other arithmetic  17.4 us (10%)
  between operations  15.1 us (9%)
  blocking collectives  13 us (8%)
    all_gather x1, waiting for transfers between devices, body(): lax.all_gather(up_weight_table, 'replica', axis=0, tiled=True)  47.4 us
    reduce_sum x2, other arithmetic, body(): totals = jnp.sum(weights, axis=-1) + jnp.sum(own_weights, axis=-1)  16.2 us
    dot_general x1, matrix products, body(): jnp.einsum('vfsgp,pvd->vfsgd', weights.astype(jnp.bfloat16), value_rows,...  15.9 us
    dot_general x1, matrix products, body(): jnp.einsum('fsvgd,pvd->vfsgp', query_heads, key_rows, preferred_element_t...  15.6 us
    unnamed x20, local copies, waits for them, and re-layouts  15.4 us
    psum x1, blocking collectives, body(): rank_activation = lax.psum(rank_activation, 'tensor')  13 us
    dot_general x1, matrix products, body(): jnp.dot(flat_rows, output_weight, preferred_element_type=jnp.float32)  11.9 us
    dot_general x1, matrix products, body(): jnp.einsum('fsvgd,ftvd->vfsgt', query_heads, new_key, preferred_element_t...  4.73 us
  transfers between devices with their start and end apart: 3, of which 1 were waited for; matrix products, arithmetic and copies ran while one was open for 53% of the time, Pallas kernels for 0%

commit v1 on v0

v1 whole, which is shorter than its diff:
```python
import functools
import math

import jax
import jax.numpy as jnp
from jax import lax
from jax.experimental import pallas as pl
from jax.experimental.pallas import tpu as pltpu
from jax.sharding import PartitionSpec as P

HD = 128
NEG = -1e30
LOG2_SCALE = math.log2(math.e) / math.sqrt(HD)
BF16, F32 = jnp.bfloat16, jnp.float32
VMEM = pl.BlockSpec(memory_space=pltpu.VMEM)
SMEM = pl.BlockSpec(memory_space=pltpu.SMEM)
PARAMS = pltpu.CompilerParams(vmem_limit_bytes=58 * 1024 * 1024)


def attention_kernel(
    unit_heads, key_block, q_ref, rk_ref, rv_ref, kv_ref, lens_ref, o_ref,
    s_a, s_b, vaug, mx_a, mx_b, mb, acc, lensb, qs,
):
    steps, forks, width = q_ref.shape
    heads = width // HD
    heads_kv = rk_ref.shape[2] // HD
    group = heads // heads_kv
    head_rows = steps * forks
    rows = unit_heads * head_rows
    units = heads // unit_heads
    prefix = kv_ref.shape[2]
    longest = jnp.max(lens_ref[...])
    blocks = (longest + (key_block - 1)) // key_block
    lens = jnp.broadcast_to(lens_ref[...], (head_rows, HD))
    for i in range(unit_heads):
        lensb[i * head_rows : (i + 1) * head_rows, :] = lens
    for v in range(heads_kv):
        vaug[v, :, 0:HD] = kv_ref[0, 1, :, v * HD : (v + 1) * HD]
        vaug[v, :, HD : 2 * HD] = jnp.ones((prefix, HD), BF16)
    for h in range(heads):
        qs[h * head_rows : (h + 1) * head_rows, :] = q_ref[:, :, h * HD : (h + 1) * HD].reshape(head_rows, HD)
    score_refs, max_refs = (s_a, s_b), (mx_a, mx_b)

    def own_scores(u, t):
        parts = []
        for i in range(unit_heads):
            h = u * unit_heads + i
            v = h // group
            k = rk_ref[t, :, v * HD : (v + 1) * HD].astype(F32)
            for s in range(steps):
                if t <= s:
                    at = h * head_rows + s * forks
                    parts.append(jnp.sum(qs[at : at + forks, :].astype(F32) * k, axis=1, keepdims=True))
                else:
                    parts.append(jnp.full((forks, 1), NEG, F32))
        return jnp.concatenate(parts, axis=0)

    def score_block(u, j, s_ref, mx_ref):
        v = (u * unit_heads) // group
        keys = kv_ref[0, 0, pl.ds(pl.multiple_of(j * key_block, key_block), key_block), v * HD : (v + 1) * HD]
        s = lax.dot_general(
            qs[u * rows : (u + 1) * rows, :], keys, (((1,), (1,)), ((), ())), preferred_element_type=F32
        )
        top = mx_ref[...]
        left = lensb[...] - j * key_block
        lane = lax.broadcasted_iota(jnp.int32, (rows, HD), 1)
        for c in range(key_block // HD):
            part = jnp.where(lane + c * HD < left, s[:, c * HD : (c + 1) * HD], NEG)
            top = jnp.maximum(top, part)
            s_ref[j, :, c * HD : (c + 1) * HD] = part
        mx_ref[...] = top

    def value_block(u, j, s_ref):
        v = (u * unit_heads) // group
        top = mb[...]
        parts = [
            jnp.exp2((s_ref[j, :, c * HD : (c + 1) * HD] - top) * LOG2_SCALE).astype(BF16)
            for c in range(key_block // HD)
        ]
        values = vaug[v, pl.ds(pl.multiple_of(j * key_block, key_block), key_block), :]
        acc[...] += jnp.dot(jnp.concatenate(parts, axis=1), values, preferred_element_type=F32)

    for u in range(units + 1):
        done = u - 1
        if u < units:
            max_refs[u % 2][...] = jnp.full((rows, HD), NEG, F32)
        if u > 0:
            own = [own_scores(done, t) for t in range(steps)]
            top = jnp.max(max_refs[done % 2][...], axis=1, keepdims=True)
            for o in own:
                top = jnp.maximum(top, o)
            mb[...] = jnp.broadcast_to(top, (rows, HD))
            acc[...] = jnp.zeros_like(acc)

        @pl.loop(0, blocks)
        def _(j):
            if u < units:
                score_block(u, j, score_refs[u % 2], max_refs[u % 2])
            if u > 0:
                value_block(done, j, score_refs[done % 2])

        if u > 0:
            weights = [jnp.exp2((o - top) * LOG2_SCALE) for o in own]
            total = acc[:, HD : 2 * HD]
            for w in weights:
                total = total + w
            for i in range(unit_heads):
                h = done * unit_heads + i
                v = h // group
                at = slice(i * head_rows, (i + 1) * head_rows)
                mixed = acc[at, 0:HD]
                for t in range(steps):
                    value = rv_ref[t, :, v * HD : (v + 1) * HD].astype(F32)
                    value = jnp.concatenate([value] * steps, axis=0)
                    mixed = mixed + weights[t][at].astype(BF16).astype(F32) * value
                o_ref[:, h * HD : (h + 1) * HD] = (mixed / total[at]).astype(BF16)


def attention(q, rk, rv, kv, lens):
    steps, forks, width = q.shape
    prefix = kv.shape[2]
    heads_kv = rk.shape[2] // HD
    unit_heads = 2
    key_block = prefix
    rows = unit_heads * steps * forks
    return pl.pallas_call(
        functools.partial(attention_kernel, unit_heads, key_block),
        out_shape=jax.ShapeDtypeStruct((steps * forks, width), BF16),
        in_specs=[VMEM] * 5,
        out_specs=VMEM,
        scratch_shapes=[pltpu.VMEM((prefix // key_block, rows, key_block), F32)] * 2
        + [pltpu.VMEM((heads_kv, prefix, 2 * HD), BF16)]
        + [pltpu.VMEM((rows, HD), F32)] * 3
        + [
            pltpu.VMEM((rows, 2 * HD), F32),
            pltpu.VMEM((rows, HD), jnp.int32),
            pltpu.VMEM((width // HD * steps * forks, HD), BF16),
        ],
        compiler_params=PARAMS,
        cost_estimate=pl.CostEstimate(flops=2 * 10**10, bytes_accessed=6 * 2**20, transcendentals=0),
        name="attention",
    )(q, rk, rv, kv, lens)


def project(attended, weight, column_group, width, add, dtype):
    rows, depth = attended.shape
    tile = 1024 if width % 1024 == 0 else width
    tiles = width // tile

    def kernel(group_ref, a_ref, w_ref, *rest):
        o_ref = rest[-1]
        part = jnp.dot(a_ref[...], w_ref[...], preferred_element_type=F32)
        if len(rest) == 2:
            part = part + rest[0][...].astype(F32)
        o_ref[...] = part.astype(o_ref.dtype)

    in_specs = [
        pl.BlockSpec((rows, depth), lambda i, g: (0, 0)),
        pl.BlockSpec((depth, tile), lambda i, g: (0, g[0] * tiles + i)),
    ]
    operands = [attended, weight]
    if add is not None:
        in_specs.append(pl.BlockSpec((rows, tile), lambda i, g: (0, i)))
        operands.append(add)
    return pl.pallas_call(
        kernel,
        out_shape=jax.ShapeDtypeStruct((rows, width), dtype),
        grid_spec=pltpu.PrefetchScalarGridSpec(
            num_scalar_prefetch=1,
            grid=(tiles,),
            in_specs=in_specs,
            out_specs=pl.BlockSpec((rows, tile), lambda i, g: (0, i)),
        ),
        compiler_params=PARAMS,
        cost_estimate=pl.CostEstimate(
            flops=2 * rows * depth * width, bytes_accessed=2 * depth * width, transcendentals=0
        ),
        name="project",
    )(column_group.reshape(1), *operands)


def pack(down, up, rows_all, place, capacity):
    replicas, batches = rows_all.shape
    stored = down.shape[0]

    def kernel(rows_ref, place_ref, down_ref, up_ref, *outs):
        me = place_ref[0]
        for d in range(1, replicas):
            to = lax.rem(me + d, replicas)
            down_out, up_out = outs[2 * (d - 1)], outs[2 * (d - 1) + 1]

            def step(b, count):
                row = rows_ref[to, b] - me * stored
                mine = (row >= 0) & (row < stored)

                @pl.when(mine)
                def _():
                    down_out[count] = down_ref[row]
                    up_out[count] = up_ref[row]

                return count + mine.astype(jnp.int32)

            lax.fori_loop(0, batches, step, jnp.int32(0))

    shapes = []
    for _ in range(1, replicas):
        shapes.append(jax.ShapeDtypeStruct((capacity,) + down.shape[1:], BF16))
        shapes.append(jax.ShapeDtypeStruct((capacity,) + up.shape[1:], BF16))
    outs = pl.pallas_call(
        kernel,
        out_shape=shapes,
        in_specs=[SMEM, SMEM, VMEM, VMEM],
        out_specs=[VMEM] * len(shapes),
        compiler_params=PARAMS,
        name="pack",
    )(rows_all, place, down, up)
    return outs[0::2], outs[1::2]


def collect(rows_ref, place_ref, replicas, table_refs, selected):
    stored = table_refs[0].shape[0]
    batches = selected.shape[0]
    me = place_ref[0]
    for d in range(replicas):
        owner = lax.rem(me + (replicas - d), replicas)
        source = table_refs[d]

        def step(b, count):
            row = rows_ref[b] - owner * stored
            there = (row >= 0) & (row < stored)

            @pl.when(there)
            def _():
                selected[b] = source[row if d == 0 else count]

            return count + there.astype(jnp.int32)

        lax.fori_loop(0, batches, step, jnp.int32(0))


def batch_mask(rows, forks, batches, rank):
    batch_forks = forks // batches
    row = lax.broadcasted_iota(jnp.int32, (rows, batches * rank), 0)
    column = lax.broadcasted_iota(jnp.int32, (rows, batches * rank), 1)
    return lax.rem(row, forks) // batch_forks == column // rank


def low_rank(attended, forks, own_rows, place, tables):
    replicas = len(tables)
    rows, depth = attended.shape
    batches = own_rows.shape[0]
    rank = tables[0].shape[1]

    def kernel(rows_ref, place_ref, a_ref, *rest):
        o_ref, selected = rest[-2], rest[-1]
        collect(rows_ref, place_ref, replicas, rest[:replicas], selected)
        every = lax.dot_general(
            a_ref[...],
            selected[...].reshape(batches * rank, depth),
            (((1,), (1,)), ((), ())),
            preferred_element_type=F32,
        )
        every = jnp.where(batch_mask(rows, forks, batches, rank), every, 0.0)
        total = every[:, 0:HD]
        for c in range(1, batches * rank // HD):
            total = total + every[:, c * HD : (c + 1) * HD]
        o_ref[...] = total

    return pl.pallas_call(
        kernel,
        out_shape=jax.ShapeDtypeStruct((rows, HD), F32),
        in_specs=[SMEM, SMEM] + [VMEM] * (1 + replicas),
        out_specs=VMEM,
        scratch_shapes=[pltpu.VMEM((batches, rank, depth), BF16)],
        compiler_params=PARAMS,
        name="low_rank",
    )(own_rows, place, attended, *tables)


def finish(base, received, ranks, forks, own_rows, place, tables):
    replicas = len(tables)
    rows, width = base.shape
    batches = own_rows.shape[0]
    rank = tables[0].shape[1]
    n_received, n_ranks = len(received), len(ranks)
    steps = rows // forks

    def kernel(rows_ref, place_ref, base_ref, *rest):
        received_refs = rest[:n_received]
        rank_refs = rest[n_received : n_received + n_ranks]
        table_refs = rest[n_received + n_ranks : -2]
        o_ref, selected = rest[-2], rest[-1]
        collect(rows_ref, place_ref, replicas, table_refs, selected)
        total = rank_refs[0][...]
        for r in rank_refs[1:]:
            total = total + r[...]
        spread = jnp.concatenate([total] * (batches * rank // HD), axis=1)
        spread = jnp.where(batch_mask(rows, forks, batches, rank), spread, 0.0)
        high = spread.astype(BF16)
        low = (spread - high.astype(F32)).astype(BF16)
        up = selected[...].reshape(batches * rank, width)
        tile = 512
        for c in range(width // tile):
            at = slice(c * tile, (c + 1) * tile)
            out = jnp.dot(high, up[:, at], preferred_element_type=F32)
            out = out + jnp.dot(low, up[:, at], preferred_element_type=F32)
            out = out + base_ref[:, at]
            for r in received_refs:
                out = out + r[:, at].astype(F32)
            o_ref[:, at] = out.astype(BF16)

    return pl.pallas_call(
        kernel,
        out_shape=jax.ShapeDtypeStruct((rows, width), BF16),
        in_specs=[SMEM, SMEM] + [VMEM] * (1 + n_received + n_ranks + replicas),
        out_specs=VMEM,
        scratch_shapes=[pltpu.VMEM((batches, rank, width), BF16)],
        compiler_params=PARAMS,
        name="finish",
    )(own_rows, place, base, *received, *ranks, *tables)


def lookup(wanted, adapter_table_row):
    matches = wanted[..., None] == jnp.arange(adapter_table_row.shape[0], dtype=jnp.int32)
    return jnp.sum(jnp.where(matches, adapter_table_row, 0), axis=-1)


def body(
    replicas,
    chips,
    queries,
    recent_keys,
    recent_values,
    prefix_key_value,
    prefix_length_each,
    batch_adapter_index,
    adapter_table_row,
    down_weight_table,
    up_weight_table,
    output_weight,
):
    forks, steps, _ = queries.shape
    batches = batch_adapter_index.shape[0]
    capacity = max(2, 2 * batches // replicas)
    model_width = output_weight.shape[1]
    width = model_width // (2 * chips)
    replica = lax.axis_index("replica").astype(jnp.int32)
    tensor = lax.axis_index("tensor").astype(jnp.int32)
    chip, core = tensor // 2, lax.rem(tensor, 2)
    place = replica.reshape(1)

    own_rows = lookup(batch_adapter_index, adapter_table_row)
    rows_all = lax.all_gather(own_rows, "replica")
    down_parts, up_parts = pack(down_weight_table, up_weight_table, rows_all, place, capacity)

    def shift(d):
        return [(z, (z + d) % replicas) for z in range(replicas)]

    downs = [lax.ppermute(down_parts[d - 1], "replica", shift(d)) for d in range(1, replicas)]
    ups = [lax.ppermute(up_parts[d - 1], "replica", shift(d)) for d in range(1, replicas)]

    lens = jnp.concatenate([prefix_length_each] * steps)[:, None]
    attended = attention(
        queries.transpose(1, 0, 2),
        recent_keys.transpose(1, 0, 2),
        recent_values.transpose(1, 0, 2),
        prefix_key_value,
        lens,
    )

    swap = [(t, t ^ 1) for t in range(2 * chips)]

    def along(e):
        return [(t, (t + 2 * e) % (2 * chips)) for t in range(2 * chips)]

    order = list(range(1, chips)) + [0]
    groups = [lax.rem(chip + e, chips) * 2 for e in order]
    halves = [
        lax.ppermute(project(attended, output_weight, g + 1 - core, width, None, BF16), "tensor", swap)
        for g in groups
    ]
    received = []
    for e, g, half in zip(order, groups, halves):
        if e:
            part = project(attended, output_weight, g + core, width, half, BF16)
            received.append(lax.ppermute(part, "tensor", along(e)))
        else:
            base = project(attended, output_weight, g + core, width, half, F32)

    rank_part = low_rank(attended, forks, own_rows, place, [down_weight_table] + downs)
    rank_chip = rank_part + lax.ppermute(rank_part, "tensor", swap)
    ranks = [rank_chip] + [lax.ppermute(rank_chip, "tensor", along(e)) for e in range(1, chips)]
    out = finish(base, received, ranks, forks, own_rows, place, [up_weight_table] + ups)
    return out.reshape(steps, forks, width).transpose(1, 0, 2)


def solution(mesh):
    placed = (
        P(("groups", "replica"), None, "tensor"),
        P(("groups", "replica"), None, "tensor"),
        P(("groups", "replica"), None, "tensor"),
        P(("groups", "replica"), None, None, "tensor"),
        P(("groups", "replica")),
        P(("groups", "replica")),
        P("groups"),
        P("replica", None, "tensor"),
        P("replica", None, "tensor"),
        P("tensor", None),
    )
    return jax.shard_map(
        functools.partial(body, mesh.shape["replica"], mesh.shape["tensor"] // 2),
        mesh=mesh,
        in_specs=placed,
        out_specs=P(("groups", "replica"), None, "tensor"),
        check_vma=False,
    )
```

time: 173 us -> 137 us (0.79)
  the two profiles are of different devices: /device:TPU:0 before, /device:TPU:9 now
where the time goes in v1:
time: 137 us
  waiting for transfers between devices  63 us (46%)
  Pallas kernels  45.5 us (33%)
  local copies, waits for them, and re-layouts  12.5 us (9%)
  starting transfers between devices  6.8 us (5%)
  blocking collectives  6.72 us (5%)
  other arithmetic  1.84 us (1%)
    ppermute x3, waiting for transfers between devices, body(): lax.ppermute(up_parts[d - 1], 'replica', shift(d))  38.7 us
    ppermute x3, waiting for transfers between devices, body(): lax.ppermute(down_parts[d - 1], 'replica', shift(d))  23.9 us
    pallas_call x1, Pallas kernels, attention(): pl.pallas_call(functools.partial(attention_kernel, unit_heads, key_block)...  16.5 us
    pallas_call x4, Pallas kernels, project(): pl.pallas_call(kernel, out_shape=jax.ShapeDtypeStruct((rows, width), dtyp...  16.4 us
    unnamed x1, blocking collectives  6.72 us
    unnamed x32, local copies, waits for them, and re-layouts  6.1 us
    pallas_call x1, Pallas kernels, finish(): pl.pallas_call(kernel, out_shape=jax.ShapeDtypeStruct((rows, width), BF16...  5.46 us
    pallas_call x1, Pallas kernels, pack(): pl.pallas_call(kernel, out_shape=shapes, in_specs=[SMEM, SMEM, VMEM, VMEM...  3.73 us
  transfers between devices with their start and end apart: 11, of which 7 were waited for; matrix products, arithmetic and copies ran while one was open for 2% of the time, Pallas kernels for 14%

profile of v1, /device:TPU:9, one launch (start us, length us, event | category | flops | bytes accessed | tf_op | source)
XLA Modules:
  0.0 137.1 jit_solution(3757830826216308757)
XLA Ops:
  0.0 0.7 pad_add_fusion
  0.7 0.8 copy.23.lens_ref
  1.5 2.0 %copy.30 = bf16[128,2,1024]{2,0,1:T(8,128)(2,1)} copy(bf16[128,2,1024]{2,1,0:T(2,128)(2,1)} %param.10) | data formatting | bytes 1048576 | tf_op args[0]
  3.5 1.7 %copy_bitcast_fusion.2 = (bf16[2,128,256]{2,1,0:T(8,128)(2,1)}, bf16[2,128,256]{2,1,0:T(8,128)(2,1)}) fusion(bf16[128,2,256]{2,1,0:T(2,128)(2,1)} %param.12, bf16[128,2,256]{2,1,0:T(2,128)(2,1)} %param.11), kind=kLoop, calls=%fused_computation.2 | loop fusion | bytes 524288 | tf_op jit(solution)/shard_map/transpose | solution.py:366
  5.2 16.5 %attention.1.a_ref = bf16[256,1024]{1,0:T(8,128)(2,1)} custom-call(bf16[2,128,1024]{2,1,0:T(8,128)(2,1)} %bitcast.19, bf16[2,128,256]{2,1,0:T(8,128)(2,1)} %get-tuple-element.18.rk_ref, bf16[2,128,256]{2,1,0:T(8,128)(2,1)} %get-tuple-element.17.rv_ref, bf16[1,2,4096,256]{3,2,1,0:T(8,128)(2,1)} %kv_ref.1, s32[256,1]{1,0:T(8,128)} %copy.23.lens_ref), custom_call_target="tpu_custom_call" | custom-call | flops 20000000000 | bytes 6291456 | tf_op jit(solution)/shard_map/attention/pallas_call | solution.py:126
  21.7 3.9 %project.6 = bf16[256,2048]{1,0:T(8,128)(2,1)} custom-call(s32[1]{0:T(128)} %bitcast.8.group_ref, bf16[256,1024]{1,0:T(8,128)(2,1)} %attention.1.a_ref, bf16[1024,8192]{1,0:T(8,128)(2,1)} %w_ref.7), custom_call_target="tpu_custom_call" | custom-call | flops 1073741824 | bytes 4194304 | tf_op jit(solution)/shard_map/project/pallas_call | solution.py:165
  25.6 0.7 collective-permute-start.1
  26.3 3.9 %project.4 = bf16[256,2048]{1,0:T(8,128)(2,1)} custom-call(s32[1]{0:T(128)} %bitcast.6.group_ref, bf16[256,1024]{1,0:T(8,128)(2,1)} %attention.1.a_ref, bf16[1024,8192]{1,0:T(8,128)(2,1)} %w_ref.7), custom_call_target="tpu_custom_call" | custom-call | flops 1073741824 | bytes 4194304 | tf_op jit(solution)/shard_map/project/pallas_call | solution.py:165
  30.2 0.0 collective-permute-start
  30.2 0.0 collective-permute-done.1.rest_0_
  30.2 1.0 copy-done.1
  31.2 4.2 %project.7 = bf16[256,2048]{1,0:T(8,128)(2,1)} custom-call(s32[1]{0:T(128)} %bitcast.7.group_ref, bf16[256,1024]{1,0:T(8,128)(2,1)} %attention.1.a_ref, bf16[1024,8192]{1,0:T(8,128)(2,1)} %w_ref.7, bf16[256,2048]{1,0:T(8,128)(2,1)} %copy-done.1), custom_call_target="tpu_custom_call" | custom-call | flops 1073741824 | bytes 4194304 | tf_op jit(solution)/shard_map/project/pallas_call | solution.py:165
  35.4 1.2 collective-permute-start.2
  36.6 0.6 dynamic-slice
  37.9 0.2 select_reduce_fusion.rows_ref
  38.1 0.2 dynamic-update-slice
  38.3 6.7 %all-reduce = s32[64]{0:T(128)S(1)} all-reduce(s32[64]{0:T(128)S(1)} %dynamic-update-slice), channel_id=2, replica_groups=mesh['groups'=2,'replica'=4,'tensor'=4] {'replica'}, use_global_device_ids=true, to_apply=%add | all-reduce | flops 64 | bytes 512
  45.0 0.7 reshape.25.rows_ref
  45.7 3.7 %pack.1 = (bf16[8,16,1024]{2,1,0:T(8,128)(2,1)}, bf16[8,16,2048]{2,1,0:T(8,128)(2,1)}, bf16[8,16,1024]{2,1,0:T(8,128)(2,1)}, bf16[8,16,2048]{2,1,0:T(8,128)(2,1)...) custom-call(s32[4,16]{1,0:T(4,128)} %reshape.25.rows_ref, s32[1]{0:T(128)} %bitcast.place_ref, ...), custom_call_target="tpu_custom_call" | custom-call | tf_op jit(solution)/shard_map/pack/pallas_call | solution.py:209
  49.4 0.0 collective-permute-start.3
  49.4 2.2 %collective-permute-start.4 = (bf16[8,16,1024]{2,1,0:T(8,128)(2,1)}, bf16[8,16,1024]{2,1,0:T(8,128)(2,1)S(1)}, u32[]{:S(2)}, u32[]{:S(2)}) collective-permute-start(bf16[8,16,1024]{2,1,0:T(8,128)(2,1)} %get-tuple-element.12), channel_id=1, source_target_pairs={{0,8},{4,12},{8,0},{12,4},{1,9},{5,13},{9,1},{13,5},{2,10},{6,14},... | collective-permute-start | bytes 786440 | tf_op jit(solution)/shard_map/ppermute | solution.py:359
  51.6 0.0 collective-permute-start.5
  51.7 3.5 %collective-permute-done.3.rest_1_ = bf16[8,16,1024]{2,1,0:T(8,128)(2,1)S(1)} collective-permute-done((bf16[8,16,1024]{2,1,0:T(8,128)(2,1)}, bf16[8,16,1024]{2,1,0:T(8,128)(2,1)S(1)}, u32[]{:S(2)}, u32[]{:S(2)}) %collective-permute-start.3) | collective-permute-done | bytes 262176 | tf_op jit(solution)/shard_map/ppermute | solution.py:359
  55.2 14.8 %collective-permute-done.4.rest_2_ = bf16[8,16,1024]{2,1,0:T(8,128)(2,1)S(1)} collective-permute-done((bf16[8,16,1024]{2,1,0:T(8,128)(2,1)}, bf16[8,16,1024]{2,1,0:T(8,128)(2,1)S(1)}, u32[]{:S(2)}, u32[]{:S(2)}) %collective-permute-start.4) | collective-permute-done | bytes 262176 | tf_op jit(solution)/shard_map/ppermute | solution.py:359
  70.0 5.5 %collective-permute-done.5.rest_3_ = bf16[8,16,1024]{2,1,0:T(8,128)(2,1)S(1)} collective-permute-done((bf16[8,16,1024]{2,1,0:T(8,128)(2,1)}, bf16[8,16,1024]{2,1,0:T(8,128)(2,1)S(1)}, u32[]{:S(2)}, u32[]{:S(2)}) %collective-permute-start.5) | collective-permute-done | bytes 262176 | tf_op jit(solution)/shard_map/ppermute | solution.py:359
  75.5 0.0 copy-done.10
  75.5 0.7 copy-done.8
  76.2 3.4 %low_rank.1 = f32[256,128]{1,0:T(8,128)} custom-call(s32[16]{0:T(128)} %copy-done.10, s32[1]{0:T(128)} %bitcast.place_ref, bf16[256,1024]{1,0:T(8,128)(2,1)} %attention.1.a_ref, bf16[16,16,1024]{2,1,0:T(8,128)(2,1)} %rest_0_.1, bf16[8,16,1024]{2,1,0:T(8,128)(2,1)} %copy-done.6, bf16[8,16,1024]{2,1,0:T(8,128)(2,1)} %copy-done.7, bf16[8,16,1024]{2,1,0:T(8,128)(2,1)} %copy-done.8), custom_call_target="tpu_custom_call" | custom-call | tf_op jit(solution)/shard_map/low_rank/pallas_call | solution.py:269
  79.6 0.5 collective-permute-start.6
  80.1 0.0 collective-permute-start.8
  80.1 0.8 collective-permute-start.9
  80.9 0.4 collective-permute-done.6
  81.3 1.1 collective-permute-start.10
  82.4 0.9 add.24.rest_1_
  83.3 0.0 collective-permute-done.rest_0_
  83.3 0.0 copy-start
  83.3 0.3 collective-permute-start.7
  83.7 0.6 copy-done
  84.3 4.3 %project.5.base_ref = f32[256,2048]{1,0:T(8,128)} custom-call(s32[1]{0:T(128)} %bitcast.1.group_ref, bf16[256,1024]{1,0:T(8,128)(2,1)} %attention.1.a_ref, bf16[1024,8192]{1,0:T(8,128)(2,1)} %w_ref.7, bf16[256,2048]{1,0:T(8,128)(2,1)} %copy-done), custom_call_target="tpu_custom_call" | custom-call | flops 1073741824 | bytes 4194304 | tf_op jit(solution)/shard_map/project/pallas_call | solution.py:165
  88.7 0.0 collective-permute-done.7.rest_2_
  88.7 5.2 %collective-permute-done.8.rest_4_ = bf16[8,16,2048]{2,1,0:T(8,128)(2,1)S(1)} collective-permute-done((bf16[8,16,2048]{2,1,0:T(8,128)(2,1)}, bf16[8,16,2048]{2,1,0:T(8,128)(2,1)S(1)}, u32[]{:S(2)}, u32[]{:S(2)}) %collective-permute-start.8) | collective-permute-done | bytes 524320 | tf_op jit(solution)/shard_map/ppermute | solution.py:360
  93.8 31.8 %collective-permute-done.9.rest_5_ = bf16[8,16,2048]{2,1,0:T(8,128)(2,1)S(1)} collective-permute-done((bf16[8,16,2048]{2,1,0:T(8,128)(2,1)}, bf16[8,16,2048]{2,1,0:T(8,128)(2,1)S(1)}, u32[]{:S(2)}, u32[]{:S(2)}) %collective-permute-start.9) | collective-permute-done | bytes 524320 | tf_op jit(solution)/shard_map/ppermute | solution.py:360
  125.7 1.7 %collective-permute-done.10.rest_6_ = bf16[8,16,2048]{2,1,0:T(8,128)(2,1)} collective-permute-done((bf16[8,16,2048]{2,1,0:T(8,128)(2,1)}, bf16[8,16,2048]{2,1,0:T(8,128)(2,1)}, u32[]{:S(2)}, u32[]{:S(2)}) %collective-permute-start.10) | collective-permute-done | bytes 524320 | tf_op jit(solution)/shard_map/ppermute | solution.py:360
  127.4 0.0 collective-permute-done.2.rest_0_
  127.4 0.0 copy-start.2
  127.4 1.0 copy-done.2
  128.4 5.5 %finish.1 = bf16[256,2048]{1,0:T(8,128)(2,1)} custom-call(s32[16]{0:T(128)} %copy-done.10, s32[1]{0:T(128)} %bitcast.place_ref, f32[256,2048]{1,0:T(8,128)} %project.5.base_ref, bf16[256,2048]{1,0:T(8,128)(2,1)} %copy-done.2, f32[256,128]{1,0:T(8,128)} %copy-done.5, f32[256,128]{1,0:T(8,128)} %copy-done.9, bf16[16,16,2048]{2,1,0:T(8,128)(2,1)} %rest_3_.1, ...), custom_call_target="tpu_custom_call" | custom-call | tf_op jit(solution)/shard_map/finish/pallas_call | solution.py:312
  133.8 3.3 %copy.29 = bf16[2,128,2048]{2,0,1:T(2,128)(2,1)} copy(bf16[2,128,2048]{2,1,0:T(8,128)(2,1)} %bitcast.18) | data formatting | bytes 2097152 | tf_op jit(solution)/shard_map/reshape | solution.py:394
  (22 shorter events, 0.0 us)
Async XLA Ops:
  25.6 4.6 %collective-permute-start.1 = (bf16[256,2048]{1,0:T(8,128)(2,1)}, bf16[256,2048]{1,0:T(8,128)(2,1)S(1)}, u32[]{:S(2)}, u32[]{:S(2)}) collective-permute-start(bf16[256,2048]{1,0:T(8,128)(2,1)} %project.6), channel_id=1, source_target_pairs={{0,1},{1,0},{2,3},{3,2},{4,5},{5,4},{6,7},{7,6},{8,9},{9,8},{10,11... | collective-permute-start | bytes 3145736 | tf_op jit(solution)/shard_map/ppermute | solution.py:379
  30.2 53.1 %collective-permute-start = (bf16[256,2048]{1,0:T(8,128)(2,1)}, bf16[256,2048]{1,0:T(8,128)(2,1)S(1)}, u32[]{:S(2)}, u32[]{:S(2)}) collective-permute-start(bf16[256,2048]{1,0:T(8,128)(2,1)} %project.4), channel_id=1, source_target_pairs={{0,1},{1,0},{2,3},{3,2},{4,5},{5,4},{6,7},{7,6},{8,9},{9,8},{10,11... | collective-permute-start | bytes 3145736 | tf_op jit(solution)/shard_map/ppermute | solution.py:379
  30.2 1.0 copy-start.1
  31.2 5.4 %copy-start.13 = (u32[32]{0:T(128)S(1)}, u32[32]{0:T(128)}, u32[]{:S(2)}) copy-start(u32[32]{0:T(128)} %constant.31) | copy-start | bytes 388
  31.2 6.7 %copy-start.11 = (s32[64]{0:T(128)S(1)}, s32[64]{0:T(128)}, u32[]{:S(2)}) copy-start(s32[64]{0:T(128)} %param.16) | copy-start | bytes 772
  31.2 6.7 %copy-start.12 = (s32[16]{0:T(128)S(1)}, s32[16]{0:T(128)}, u32[]{:S(2)}) copy-start(s32[16]{0:T(128)} %param.15) | copy-start | bytes 196
  35.4 92.0 %collective-permute-start.2 = (bf16[256,2048]{1,0:T(8,128)(2,1)}, bf16[256,2048]{1,0:T(8,128)(2,1)S(1)}, u32[]{:S(2)}, u32[]{:S(2)}) collective-permute-start(bf16[256,2048]{1,0:T(8,128)(2,1)} %project.7), channel_id=1, source_target_pairs={{0,2},{1,3},{2,0},{3,1},{4,6},{5,7},{6,4},{7,5},{8,10},{9,11},{10,... | collective-permute-start | bytes 3145736 | tf_op jit(solution)/shard_map/ppermute | solution.py:386
  38.1 37.4 %copy-start.10 = (s32[16]{0:T(128)}, s32[16]{0:T(128)S(1)}, u32[]{:S(2)}) copy-start(s32[16]{0:T(128)S(1)} %select_reduce_fusion.rows_ref) | copy-start | bytes 196
  49.4 5.7 %collective-permute-start.3 = (bf16[8,16,1024]{2,1,0:T(8,128)(2,1)}, bf16[8,16,1024]{2,1,0:T(8,128)(2,1)S(1)}, u32[]{:S(2)}, u32[]{:S(2)}) collective-permute-start(bf16[8,16,1024]{2,1,0:T(8,128)(2,1)} %get-tuple-element.11), channel_id=1, source_target_pairs={{0,4},{4,8},{8,12},{12,0},{1,5},{5,9},{9,13},{13,1},{2,6},{6,10},{... | collective-permute-start | bytes 786440 | tf_op jit(solution)/shard_map/ppermute | solution.py:359
  49.4 20.5 %collective-permute-start.4 = (bf16[8,16,1024]{2,1,0:T(8,128)(2,1)}, bf16[8,16,1024]{2,1,0:T(8,128)(2,1)S(1)}, u32[]{:S(2)}, u32[]{:S(2)}) collective-permute-start(bf16[8,16,1024]{2,1,0:T(8,128)(2,1)} %get-tuple-element.12), channel_id=1, source_target_pairs={{0,8},{4,12},{8,0},{12,4},{1,9},{5,13},{9,1},{13,5},{2,10},{6,14},... | collective-permute-start | bytes 786440 | tf_op jit(solution)/shard_map/ppermute | solution.py:359
  51.6 23.9 %collective-permute-start.5 = (bf16[8,16,1024]{2,1,0:T(8,128)(2,1)}, bf16[8,16,1024]{2,1,0:T(8,128)(2,1)S(1)}, u32[]{:S(2)}, u32[]{:S(2)}) collective-permute-start(bf16[8,16,1024]{2,1,0:T(8,128)(2,1)} %get-tuple-element.13), channel_id=1, source_target_pairs={{0,12},{4,0},{8,4},{12,8},{1,13},{5,1},{9,5},{13,9},{2,14},{6,2},{... | collective-permute-start | bytes 786440 | tf_op jit(solution)/shard_map/ppermute | solution.py:359
  55.2 20.4 %copy-start.6 = (bf16[8,16,1024]{2,1,0:T(8,128)(2,1)}, bf16[8,16,1024]{2,1,0:T(8,128)(2,1)S(1)}, u32[]{:S(2)}) copy-start(bf16[8,16,1024]{2,1,0:T(8,128)(2,1)S(1)} %collective-permute-done.3.rest_1_) | copy-start | bytes 786436
  70.0 5.5 %copy-start.7 = (bf16[8,16,1024]{2,1,0:T(8,128)(2,1)}, bf16[8,16,1024]{2,1,0:T(8,128)(2,1)S(1)}, u32[]{:S(2)}) copy-start(bf16[8,16,1024]{2,1,0:T(8,128)(2,1)S(1)} %collective-permute-done.4.rest_2_) | copy-start | bytes 786436
  75.5 0.7 copy-start.8
  79.6 1.7 %collective-permute-start.6 = (f32[256,128]{1,0:T(8,128)}, f32[256,128]{1,0:T(8,128)S(1)}, u32[]{:S(2)}, u32[]{:S(2)}) collective-permute-start(f32[256,128]{1,0:T(8,128)} %low_rank.1), channel_id=1, source_target_pairs={{0,1},{1,0},{2,3},{3,2},{4,5},{5,4},{6,7},{7,6},{8,9},{9,8},{10,11... | collective-permute-start | bytes 393224 | tf_op jit(solution)/shard_map/ppermute | solution.py:391
  80.1 13.7 %collective-permute-start.8 = (bf16[8,16,2048]{2,1,0:T(8,128)(2,1)}, bf16[8,16,2048]{2,1,0:T(8,128)(2,1)S(1)}, u32[]{:S(2)}, u32[]{:S(2)}) collective-permute-start(bf16[8,16,2048]{2,1,0:T(8,128)(2,1)} %get-tuple-element.14), channel_id=1, source_target_pairs={{0,4},{4,8},{8,12},{12,0},{1,5},{5,9},{9,13},{13,1},{2,6},{6,10},{... | collective-permute-start | bytes 1572872 | tf_op jit(solution)/shard_map/ppermute | solution.py:360
  80.1 45.6 %collective-permute-start.9 = (bf16[8,16,2048]{2,1,0:T(8,128)(2,1)}, bf16[8,16,2048]{2,1,0:T(8,128)(2,1)S(1)}, u32[]{:S(2)}, u32[]{:S(2)}) collective-permute-start(bf16[8,16,2048]{2,1,0:T(8,128)(2,1)} %get-tuple-element.15), channel_id=1, source_target_pairs={{0,8},{4,12},{8,0},{12,4},{1,9},{5,13},{9,1},{13,5},{2,10},{6,14},... | collective-permute-start | bytes 1572872 | tf_op jit(solution)/shard_map/ppermute | solution.py:360
  81.3 46.1 %collective-permute-start.10 = (bf16[8,16,2048]{2,1,0:T(8,128)(2,1)}, bf16[8,16,2048]{2,1,0:T(8,128)(2,1)}, u32[]{:S(2)}, u32[]{:S(2)}) collective-permute-start(bf16[8,16,2048]{2,1,0:T(8,128)(2,1)} %get-tuple-element.16), channel_id=1, source_target_pairs={{0,12},{4,0},{8,4},{12,8},{1,13},{5,1},{9,5},{13,9},{2,14},{6,2},{... | collective-permute-start | bytes 1572872 | tf_op jit(solution)/shard_map/ppermute | solution.py:360
  83.3 44.1 %copy-start.5 = (f32[256,128]{1,0:T(8,128)}, f32[256,128]{1,0:T(8,128)S(1)}, u32[]{:S(2)}) copy-start(f32[256,128]{1,0:T(8,128)S(1)} %add.24.rest_1_) | copy-start | bytes 393220
  83.3 1.0 copy-start
  83.3 5.3 %collective-permute-start.7 = (f32[256,128]{1,0:T(8,128)S(1)}, f32[256,128]{1,0:T(8,128)S(1)}, u32[]{:S(2)}, u32[]{:S(2)}) collective-permute-start(f32[256,128]{1,0:T(8,128)S(1)} %add.24.rest_1_), channel_id=1, source_target_pairs={{0,2},{1,3},{2,0},{3,1},{4,6},{5,7},{6,4},{7,5},{8,10},{9,11},{10,... | collective-permute-start | bytes 393224 | tf_op jit(solution)/shard_map/ppermute | solution.py:392
  88.7 38.7 %copy-start.9 = (f32[256,128]{1,0:T(8,128)}, f32[256,128]{1,0:T(8,128)S(1)}, u32[]{:S(2)}) copy-start(f32[256,128]{1,0:T(8,128)S(1)} %collective-permute-done.7.rest_2_) | copy-start | bytes 393220
  93.8 33.5 %copy-start.3 = (bf16[8,16,2048]{2,1,0:T(8,128)(2,1)}, bf16[8,16,2048]{2,1,0:T(8,128)(2,1)S(1)}, u32[]{:S(2)}) copy-start(bf16[8,16,2048]{2,1,0:T(8,128)(2,1)S(1)} %collective-permute-done.8.rest_4_) | copy-start | bytes 1572868
  125.7 1.7 %copy-start.4 = (bf16[8,16,2048]{2,1,0:T(8,128)(2,1)}, bf16[8,16,2048]{2,1,0:T(8,128)(2,1)S(1)}, u32[]{:S(2)}) copy-start(bf16[8,16,2048]{2,1,0:T(8,128)(2,1)S(1)} %collective-permute-done.9.rest_5_) | copy-start | bytes 1572868
  127.4 1.0 copy-start.2

commit v2 on v1

--- a/solution.py
+++ b/solution.py
@@ -181,13 +181,14 @@
 
 def pack(down, up, rows_all, place, capacity):
     replicas, batches = rows_all.shape
-    stored = down.shape[0]
+    stored, rank, up_width = up.shape
+    width = up_width + down.shape[2]
 
     def kernel(rows_ref, place_ref, down_ref, up_ref, *outs):
         me = place_ref[0]
         for d in range(1, replicas):
             to = lax.rem(me + d, replicas)
-            down_out, up_out = outs[2 * (d - 1)], outs[2 * (d - 1) + 1]
+            out = outs[d - 1]
 
             def step(b, count):
                 row = rows_ref[to, b] - me * stored
@@ -195,26 +196,21 @@
 
                 @pl.when(mine)
                 def _():
-                    down_out[count] = down_ref[row]
-                    up_out[count] = up_ref[row]
+                    out[count, :, 0:up_width] = up_ref[row]
+                    out[count, :, up_width:width] = down_ref[row]
 
                 return count + mine.astype(jnp.int32)
 
             lax.fori_loop(0, batches, step, jnp.int32(0))
 
-    shapes = []
-    for _ in range(1, replicas):
-        shapes.append(jax.ShapeDtypeStruct((capacity,) + down.shape[1:], BF16))
-        shapes.append(jax.ShapeDtypeStruct((capacity,) + up.shape[1:], BF16))
-    outs = pl.pallas_call(
+    return pl.pallas_call(
         kernel,
-        out_shape=shapes,
+        out_shape=[jax.ShapeDtypeStruct((capacity, rank, width), BF16)] * (replicas - 1),
         in_specs=[SMEM, SMEM, VMEM, VMEM],
-        out_specs=[VMEM] * len(shapes),
+        out_specs=[VMEM] * (replicas - 1),
         compiler_params=PARAMS,
         name="pack",
     )(rows_all, place, down, up)
-    return outs[0::2], outs[1::2]
 
 
 def collect(rows_ref, place_ref, replicas, table_refs, selected):
@@ -236,6 +232,15 @@
             return count + there.astype(jnp.int32)
 
         lax.fori_loop(0, batches, step, jnp.int32(0))
+
+
+def whole(shape):
+    return pl.BlockSpec(shape, lambda i: (0,) * len(shape))
+
+
+def columns(packed, width, block):
+    shape = packed.shape[:-1] + (width,)
+    return pl.BlockSpec(shape, lambda i: (0,) * (len(shape) - 1) + (block,))
 
 
 def batch_mask(rows, forks, batches, rank):
@@ -269,8 +274,10 @@
     return pl.pallas_call(
         kernel,
         out_shape=jax.ShapeDtypeStruct((rows, HD), F32),
-        in_specs=[SMEM, SMEM] + [VMEM] * (1 + replicas),
-        out_specs=VMEM,
+        grid=(1,),
+        in_specs=[SMEM, SMEM, whole(attended.shape), whole(tables[0].shape)]
+        + [columns(t, depth, (t.shape[2] - depth) // depth) for t in tables[1:]],
+        out_specs=whole((rows, HD)),
         scratch_shapes=[pltpu.VMEM((batches, rank, depth), BF16)],
         compiler_params=PARAMS,
         name="low_rank",
@@ -312,8 +319,11 @@
     return pl.pallas_call(
         kernel,
         out_shape=jax.ShapeDtypeStruct((rows, width), BF16),
-        in_specs=[SMEM, SMEM] + [VMEM] * (1 + n_received + n_ranks + replicas),
-        out_specs=VMEM,
+        grid=(1,),
+        in_specs=[SMEM, SMEM]
+        + [whole(x.shape) for x in (base, *received, *ranks, tables[0])]
+        + [columns(t, width, 0) for t in tables[1:]],
+        out_specs=whole((rows, width)),
         scratch_shapes=[pltpu.VMEM((batches, rank, width), BF16)],
         compiler_params=PARAMS,
         name="finish",
@@ -351,13 +361,12 @@
 
     own_rows = lookup(batch_adapter_index, adapter_table_row)
     rows_all = lax.all_gather(own_rows, "replica")
-    down_parts, up_parts = pack(down_weight_table, up_weight_table, rows_all, place, capacity)
-
-    def shift(d):
-        return [(z, (z + d) % replicas) for z in range(replicas)]
-
-    downs = [lax.ppermute(down_parts[d - 1], "replica", shift(d)) for d in range(1, replicas)]
-    ups = [lax.ppermute(up_parts[d - 1], "replica", shift(d)) for d in range(1, replicas)]
+    parts = pack(down_weight_table, up_weight_table, rows_all, place, capacity)
+    queries = lax.optimization_barrier((queries, *parts))[0]
+    arrived = [
+        lax.ppermute(parts[d - 1], "replica", [(z, (z + d) % replicas) for z in range(replicas)])
+        for d in range(1, replicas)
+    ]
 
     lens = jnp.concatenate([prefix_length_each] * steps)[:, None]
     attended = attention(
@@ -387,10 +396,10 @@
         else:
             base = project(attended, output_weight, g + core, width, half, F32)
 
-    rank_part = low_rank(attended, forks, own_rows, place, [down_weight_table] + downs)
+    rank_part = low_rank(attended, forks, own_rows, place, [down_weight_table] + arrived)
     rank_chip = rank_part + lax.ppermute(rank_part, "tensor", swap)
     ranks = [rank_chip] + [lax.ppermute(rank_chip, "tensor", along(e)) for e in range(1, chips)]
-    out = finish(base, received, ranks, forks, own_rows, place, [up_weight_table] + ups)
+    out = finish(base, received, ranks, forks, own_rows, place, [up_weight_table] + arrived)
     return out.reshape(steps, forks, width).transpose(1, 0, 2)
 
 

time: 137 us -> 136 us (level)
  the two profiles are of different devices: /device:TPU:9 before, /device:TPU:13 now
where the time goes in v2:
time: 136 us
  waiting for transfers between devices  59.2 us (44%)
  Pallas kernels  45.5 us (33%)
  local copies, waits for them, and re-layouts  13.4 us (10%)
  starting transfers between devices  8.49 us (6%)
  blocking collectives  6.43 us (5%)
  other arithmetic  2.51 us (2%)
    ppermute x3, waiting for transfers between devices, body(): lax.ppermute(parts[d - 1], 'replica', [(z, (z + d) % replicas) for z in r...  58 us
    pallas_call x1, Pallas kernels, attention(): pl.pallas_call(functools.partial(attention_kernel, unit_heads, key_block)...  16.5 us
    pallas_call x4, Pallas kernels, project(): pl.pallas_call(kernel, out_shape=jax.ShapeDtypeStruct((rows, width), dtyp...  16.4 us
    unnamed x1, blocking collectives  6.43 us
    pallas_call x1, Pallas kernels, finish(): pl.pallas_call(kernel, out_shape=jax.ShapeDtypeStruct((rows, width), BF16...  5.44 us
    unnamed x19, local copies, waits for them, and re-layouts  4.97 us
    pallas_call x1, Pallas kernels, pack(): pl.pallas_call(kernel, out_shape=[jax.ShapeDtypeStruct((capacity, rank, w...  3.68 us
    pallas_call x1, Pallas kernels, low_rank(): pl.pallas_call(kernel, out_shape=jax.ShapeDtypeStruct((rows, HD), F32), g...  3.43 us
  transfers between devices with their start and end apart: 8, of which 4 were waited for; matrix products, arithmetic and copies ran while one was open for 1% of the time, Pallas kernels for 12%

profile of v2, /device:TPU:13, one launch (start us, length us, event | category | flops | bytes accessed | tf_op | source)
XLA Modules:
  0.0 136.1 jit_solution(15515916066230002471)
XLA Ops:
  0.0 0.9 select_reduce_fusion.rows_ref
  0.9 0.0 copy-start.7
  0.9 1.2 dynamic-slice
  2.8 0.2 dynamic-update-slice
  3.0 6.4 %all-reduce = s32[64]{0:T(128)S(1)} all-reduce(s32[64]{0:T(128)S(1)} %dynamic-update-slice), channel_id=2, replica_groups=mesh['groups'=2,'replica'=4,'tensor'=4] {'replica'}, use_global_device_ids=true, to_apply=%add | all-reduce | flops 64 | bytes 512
  9.4 0.7 reshape.25.rows_ref
  10.1 3.7 %pack.1 = (bf16[8,16,3072]{2,1,0:T(8,128)(2,1)}, bf16[8,16,3072]{2,1,0:T(8,128)(2,1)}, bf16[8,16,3072]{2,1,0:T(8,128)(2,1)}) custom-call(s32[4,16]{1,0:T(4,128)} %reshape.25.rows_ref, s32[1]{0:T(128)} %bitcast.place_ref, bf16[16,16,1024]{2,1,0:T(8,128)(2,1)} %rest_0_.1, bf16[16,16,2048]{2,1,0:T(8,128)(2,1)} %rest_3_.1), custom_call_target="tpu_custom_call" | custom-call | tf_op jit(solution)/shard_map/pack/pallas_call | solution.py:206
  13.8 2.0 %copy.30 = bf16[128,2,1024]{2,0,1:T(8,128)(2,1)} copy(bf16[128,2,1024]{2,1,0:T(2,128)(2,1)} %param.10) | data formatting | bytes 1048576 | tf_op jit(solution)/shard_map/optimization_barrier | solution.py:365
  15.7 0.7 pad_add_fusion
  16.5 0.8 copy.23.lens_ref
  17.3 1.7 %copy_bitcast_fusion.2 = (bf16[2,128,256]{2,1,0:T(8,128)(2,1)}, bf16[2,128,256]{2,1,0:T(8,128)(2,1)}) fusion(bf16[128,2,256]{2,1,0:T(2,128)(2,1)} %param.12, bf16[128,2,256]{2,1,0:T(2,128)(2,1)} %param.11), kind=kLoop, calls=%fused_computation.2 | loop fusion | bytes 524288 | tf_op jit(solution)/shard_map/transpose | solution.py:375
  19.0 16.5 %attention.1.a_ref = bf16[256,1024]{1,0:T(8,128)(2,1)} custom-call(bf16[2,128,1024]{2,1,0:T(8,128)(2,1)} %bitcast.19, bf16[2,128,256]{2,1,0:T(8,128)(2,1)} %get-tuple-element.14.rk_ref, bf16[2,128,256]{2,1,0:T(8,128)(2,1)} %get-tuple-element.13.rv_ref, bf16[1,2,4096,256]{3,2,1,0:T(8,128)(2,1)} %kv_ref.1, s32[256,1]{1,0:T(8,128)} %copy.23.lens_ref), custom_call_target="tpu_custom_call" | custom-call | flops 20000000000 | bytes 6291456 | tf_op jit(solution)/shard_map/attention/pallas_call | solution.py:126
  35.5 0.0 copy-done.7
  35.5 4.0 %project.6 = bf16[256,2048]{1,0:T(8,128)(2,1)} custom-call(s32[1]{0:T(128)} %bitcast.9.group_ref, bf16[256,1024]{1,0:T(8,128)(2,1)} %attention.1.a_ref, bf16[1024,8192]{1,0:T(8,128)(2,1)} %w_ref.7), custom_call_target="tpu_custom_call" | custom-call | flops 1073741824 | bytes 4194304 | tf_op jit(solution)/shard_map/project/pallas_call | solution.py:165
  39.5 2.7 %collective-permute-start.1 = (bf16[256,2048]{1,0:T(8,128)(2,1)}, bf16[256,2048]{1,0:T(8,128)(2,1)S(1)}, u32[]{:S(2)}, u32[]{:S(2)}) collective-permute-start(bf16[256,2048]{1,0:T(8,128)(2,1)} %project.6), channel_id=1, source_target_pairs={{0,1},{1,0},{2,3},{3,2},{4,5},{5,4},{6,7},{7,6},{8,9},{9,8},{10,11... | collective-permute-start | bytes 3145736 | tf_op jit(solution)/shard_map/ppermute | solution.py:388
  42.1 0.0 collective-permute-start.3
  42.1 2.3 %collective-permute-start.4 = (bf16[8,16,3072]{2,1,0:T(8,128)(2,1)}, bf16[8,16,3072]{2,1,0:T(8,128)(2,1)S(1)}, u32[]{:S(2)}, u32[]{:S(2)}) collective-permute-start(bf16[8,16,3072]{2,1,0:T(8,128)(2,1)} %get-tuple-element.10), channel_id=1, source_target_pairs={{0,8},{4,12},{8,0},{12,4},{1,9},{5,13},{9,1},{13,5},{2,10},{6,14},... | collective-permute-start | bytes 2359304 | tf_op jit(solution)/shard_map/ppermute | solution.py:367
  44.4 0.0 collective-permute-start.5
  44.4 3.9 %project.4 = bf16[256,2048]{1,0:T(8,128)(2,1)} custom-call(s32[1]{0:T(128)} %bitcast.7.group_ref, bf16[256,1024]{1,0:T(8,128)(2,1)} %attention.1.a_ref, bf16[1024,8192]{1,0:T(8,128)(2,1)} %w_ref.7), custom_call_target="tpu_custom_call" | custom-call | flops 1073741824 | bytes 4194304 | tf_op jit(solution)/shard_map/project/pallas_call | solution.py:165
  48.3 0.6 collective-permute-start
  48.9 0.0 collective-permute-done.1.rest_0_
  48.9 0.0 copy-start.4
  48.9 1.0 copy-done.4
  49.9 4.2 %project.7 = bf16[256,2048]{1,0:T(8,128)(2,1)} custom-call(s32[1]{0:T(128)} %bitcast.8.group_ref, bf16[256,1024]{1,0:T(8,128)(2,1)} %attention.1.a_ref, bf16[1024,8192]{1,0:T(8,128)(2,1)} %w_ref.7, bf16[256,2048]{1,0:T(8,128)(2,1)} %copy-done.4), custom_call_target="tpu_custom_call" | custom-call | flops 1073741824 | bytes 4194304 | tf_op jit(solution)/shard_map/project/pallas_call | solution.py:165
  54.0 1.2 collective-permute-start.2
  55.3 6.3 %collective-permute-done.3.rest_1_.rest_4_ = bf16[8,16,3072]{2,1,0:T(8,128)(2,1)S(1)} collective-permute-done((bf16[8,16,3072]{2,1,0:T(8,128)(2,1)}, bf16[8,16,3072]{2,1,0:T(8,128)(2,1)S(1)}, u32[]{:S(2)}, u32[]{:S(2)}) %collective-permute-start.3) | collective-permute-done | bytes 786464 | tf_op jit(solution)/shard_map/ppermute | solution.py:367
  61.5 0.0 copy-start
  61.5 48.7 %collective-permute-done.4.rest_2_.rest_5_ = bf16[8,16,3072]{2,1,0:T(8,128)(2,1)S(1)} collective-permute-done((bf16[8,16,3072]{2,1,0:T(8,128)(2,1)}, bf16[8,16,3072]{2,1,0:T(8,128)(2,1)S(1)}, u32[]{:S(2)}, u32[]{:S(2)}) %collective-permute-start.4) | collective-permute-done | bytes 786464 | tf_op jit(solution)/shard_map/ppermute | solution.py:367
  110.2 3.0 %collective-permute-done.5.rest_3_.rest_6_ = bf16[8,16,3072]{2,1,0:T(8,128)(2,1)S(1)} collective-permute-done((bf16[8,16,3072]{2,1,0:T(8,128)(2,1)}, bf16[8,16,3072]{2,1,0:T(8,128)(2,1)S(1)}, u32[]{:S(2)}, u32[]{:S(2)}) %collective-permute-start.5) | collective-permute-done | bytes 786464 | tf_op jit(solution)/shard_map/ppermute | solution.py:367
  113.2 0.0 copy-done
  113.2 0.0 copy-done.1
  113.3 0.9 copy-done.2
  114.1 3.4 %low_rank.1 = f32[256,128]{1,0:T(8,128)} custom-call(s32[16]{0:T(128)} %copy-done.7, s32[1]{0:T(128)} %bitcast.place_ref, bf16[256,1024]{1,0:T(8,128)(2,1)} %attention.1.a_ref, bf16[16,16,1024]{2,1,0:T(8,128)(2,1)} %rest_0_.1, bf16[8,16,3072]{2,1,0:T(8,128)(2,1)} %copy-done, bf16[8,16,3072]{2,1,0:T(8,128)(2,1)} %copy-done.1, bf16[8,16,3072]{2,1,0:T(8,128)(2,1)} %copy-done.2), custom_call_target="tpu_custom_call" | custom-call | tf_op jit(solution)/shard_map/low_rank/pallas_call | solution.py:274
  117.6 0.5 collective-permute-start.6
  118.0 1.2 collective-permute-done.6
  119.2 0.9 add.24.rest_1_
  120.2 0.0 copy-start.5
  120.2 1.3 collective-permute-start.7
  121.5 0.0 collective-permute-done.rest_0_
  121.5 4.3 %project.5.base_ref = f32[256,2048]{1,0:T(8,128)} custom-call(s32[1]{0:T(128)} %bitcast.1.group_ref, bf16[256,1024]{1,0:T(8,128)(2,1)} %attention.1.a_ref, bf16[1024,8192]{1,0:T(8,128)(2,1)} %w_ref.7, bf16[256,2048]{1,0:T(8,128)(2,1)} %collective-permute-done.rest_0_), custom_call_target="tpu_custom_call" | custom-call | flops 1073741824 | bytes 4194304 | tf_op jit(solution)/shard_map/project/pallas_call | solution.py:165
  125.8 0.0 copy-done.5
  125.8 0.0 collective-permute-done.7.rest_2_
  125.8 0.0 copy-start.6
  125.8 0.0 collective-permute-done.2.rest_0_
  125.8 0.6 copy-done.6
  126.5 1.0 copy-done.3
  127.4 5.4 %finish.1 = bf16[256,2048]{1,0:T(8,128)(2,1)} custom-call(s32[16]{0:T(128)} %copy-done.7, s32[1]{0:T(128)} %bitcast.place_ref, f32[256,2048]{1,0:T(8,128)} %project.5.base_ref, bf16[256,2048]{1,0:T(8,128)(2,1)} %copy-done.3, f32[256,128]{1,0:T(8,128)} %copy-done.5, f32[256,128]{1,0:T(8,128)} %copy-done.6, bf16[16,16,2048]{2,1,0:T(8,128)(2,1)} %rest_3_.1, ...), custom_call_target="tpu_custom_call" | custom-call | tf_op jit(solution)/shard_map/finish/pallas_call | solution.py:319
  132.9 3.3 %copy.29 = bf16[2,128,2048]{2,0,1:T(2,128)(2,1)} copy(bf16[2,128,2048]{2,1,0:T(8,128)(2,1)} %bitcast.18) | data formatting | bytes 2097152 | tf_op jit(solution)/shard_map/reshape | solution.py:403
  (4 shorter events, 0.0 us)
Async XLA Ops:
  0.9 34.6 %copy-start.7 = (s32[16]{0:T(128)}, s32[16]{0:T(128)S(1)}, u32[]{:S(2)}) copy-start(s32[16]{0:T(128)S(1)} %select_reduce_fusion.rows_ref) | copy-start | bytes 196
  39.5 9.4 %collective-permute-start.1 = (bf16[256,2048]{1,0:T(8,128)(2,1)}, bf16[256,2048]{1,0:T(8,128)(2,1)S(1)}, u32[]{:S(2)}, u32[]{:S(2)}) collective-permute-start(bf16[256,2048]{1,0:T(8,128)(2,1)} %project.6), channel_id=1, source_target_pairs={{0,1},{1,0},{2,3},{3,2},{4,5},{5,4},{6,7},{7,6},{8,9},{9,8},{10,11... | collective-permute-start | bytes 3145736 | tf_op jit(solution)/shard_map/ppermute | solution.py:388
  42.1 19.4 %collective-permute-start.3 = (bf16[8,16,3072]{2,1,0:T(8,128)(2,1)}, bf16[8,16,3072]{2,1,0:T(8,128)(2,1)S(1)}, u32[]{:S(2)}, u32[]{:S(2)}) collective-permute-start(bf16[8,16,3072]{2,1,0:T(8,128)(2,1)} %get-tuple-element.9), channel_id=1, source_target_pairs={{0,4},{4,8},{8,12},{12,0},{1,5},{5,9},{9,13},{13,1},{2,6},{6,10},{... | collective-permute-start | bytes 2359304 | tf_op jit(solution)/shard_map/ppermute | solution.py:367
  42.1 68.0 %collective-permute-start.4 = (bf16[8,16,3072]{2,1,0:T(8,128)(2,1)}, bf16[8,16,3072]{2,1,0:T(8,128)(2,1)S(1)}, u32[]{:S(2)}, u32[]{:S(2)}) collective-permute-start(bf16[8,16,3072]{2,1,0:T(8,128)(2,1)} %get-tuple-element.10), channel_id=1, source_target_pairs={{0,8},{4,12},{8,0},{12,4},{1,9},{5,13},{9,1},{13,5},{2,10},{6,14},... | collective-permute-start | bytes 2359304 | tf_op jit(solution)/shard_map/ppermute | solution.py:367
  44.4 68.8 %collective-permute-start.5 = (bf16[8,16,3072]{2,1,0:T(8,128)(2,1)}, bf16[8,16,3072]{2,1,0:T(8,128)(2,1)S(1)}, u32[]{:S(2)}, u32[]{:S(2)}) collective-permute-start(bf16[8,16,3072]{2,1,0:T(8,128)(2,1)} %get-tuple-element.11), channel_id=1, source_target_pairs={{0,12},{4,0},{8,4},{12,8},{1,13},{5,1},{9,5},{13,9},{2,14},{6,2},{... | collective-permute-start | bytes 2359304 | tf_op jit(solution)/shard_map/ppermute | solution.py:367
  48.3 73.1 %collective-permute-start = (bf16[256,2048]{1,0:T(8,128)(2,1)}, bf16[256,2048]{1,0:T(8,128)(2,1)}, u32[]{:S(2)}, u32[]{:S(2)}) collective-permute-start(bf16[256,2048]{1,0:T(8,128)(2,1)} %project.4), channel_id=1, source_target_pairs={{0,1},{1,0},{2,3},{3,2},{4,5},{5,4},{6,7},{7,6},{8,9},{9,8},{10,11... | collective-permute-start | bytes 3145736 | tf_op jit(solution)/shard_map/ppermute | solution.py:388
  48.9 1.0 copy-start.4
  54.0 71.8 %collective-permute-start.2 = (bf16[256,2048]{1,0:T(8,128)(2,1)}, bf16[256,2048]{1,0:T(8,128)(2,1)S(1)}, u32[]{:S(2)}, u32[]{:S(2)}) collective-permute-start(bf16[256,2048]{1,0:T(8,128)(2,1)} %project.7), channel_id=1, source_target_pairs={{0,2},{1,3},{2,0},{3,1},{4,6},{5,7},{6,4},{7,5},{8,10},{9,11},{10,... | collective-permute-start | bytes 3145736 | tf_op jit(solution)/shard_map/ppermute | solution.py:395
  61.5 51.7 %copy-start = (bf16[8,16,3072]{2,1,0:T(8,128)(2,1)}, bf16[8,16,3072]{2,1,0:T(8,128)(2,1)S(1)}, u32[]{:S(2)}) copy-start(bf16[8,16,3072]{2,1,0:T(8,128)(2,1)S(1)} %collective-permute-done.3.rest_1_.rest_4_) | copy-start | bytes 2359300
  110.2 3.1 %copy-start.1 = (bf16[8,16,3072]{2,1,0:T(8,128)(2,1)}, bf16[8,16,3072]{2,1,0:T(8,128)(2,1)S(1)}, u32[]{:S(2)}) copy-start(bf16[8,16,3072]{2,1,0:T(8,128)(2,1)S(1)} %collective-permute-done.4.rest_2_.rest_5_) | copy-start | bytes 2359300
  113.3 0.9 copy-start.2
  117.6 1.7 %collective-permute-start.6 = (f32[256,128]{1,0:T(8,128)}, f32[256,128]{1,0:T(8,128)S(1)}, u32[]{:S(2)}, u32[]{:S(2)}) collective-permute-start(f32[256,128]{1,0:T(8,128)} %low_rank.1), channel_id=1, source_target_pairs={{0,1},{1,0},{2,3},{3,2},{4,5},{5,4},{6,7},{7,6},{8,9},{9,8},{10,11... | collective-permute-start | bytes 393224 | tf_op jit(solution)/shard_map/ppermute | solution.py:400
  120.2 5.7 %copy-start.5 = (f32[256,128]{1,0:T(8,128)}, f32[256,128]{1,0:T(8,128)S(1)}, u32[]{:S(2)}) copy-start(f32[256,128]{1,0:T(8,128)S(1)} %add.24.rest_1_) | copy-start | bytes 393220
  120.2 5.6 %collective-permute-start.7 = (f32[256,128]{1,0:T(8,128)S(1)}, f32[256,128]{1,0:T(8,128)S(1)}, u32[]{:S(2)}, u32[]{:S(2)}) collective-permute-start(f32[256,128]{1,0:T(8,128)S(1)} %add.24.rest_1_), channel_id=1, source_target_pairs={{0,2},{1,3},{2,0},{3,1},{4,6},{5,7},{6,4},{7,5},{8,10},{9,11},{10,... | collective-permute-start | bytes 393224 | tf_op jit(solution)/shard_map/ppermute | solution.py:401
  125.8 0.7 copy-start.6
  126.5 1.0 copy-start.3

commit v3 on v2

--- a/solution.py
+++ b/solution.py
@@ -184,11 +184,9 @@
     stored, rank, up_width = up.shape
     width = up_width + down.shape[2]
 
-    def kernel(rows_ref, place_ref, down_ref, up_ref, *outs):
+    def kernel(rows_ref, place_ref, down_ref, up_ref, out):
         me = place_ref[0]
-        for d in range(1, replicas):
-            to = lax.rem(me + d, replicas)
-            out = outs[d - 1]
+        for to in range(replicas):
 
             def step(b, count):
                 row = rows_ref[to, b] - me * stored
@@ -196,8 +194,8 @@
 
                 @pl.when(mine)
                 def _():
-                    out[count, :, 0:up_width] = up_ref[row]
-                    out[count, :, up_width:width] = down_ref[row]
+                    out[to, count, :, 0:up_width] = up_ref[row]
+                    out[to, count, :, up_width:width] = down_ref[row]
 
                 return count + mine.astype(jnp.int32)
 
@@ -205,21 +203,17 @@
 
     return pl.pallas_call(
         kernel,
-        out_shape=[jax.ShapeDtypeStruct((capacity, rank, width), BF16)] * (replicas - 1),
+        out_shape=jax.ShapeDtypeStruct((replicas, capacity, rank, width), BF16),
         in_specs=[SMEM, SMEM, VMEM, VMEM],
-        out_specs=[VMEM] * (replicas - 1),
+        out_specs=VMEM,
         compiler_params=PARAMS,
         name="pack",
     )(rows_all, place, down, up)
 
 
-def collect(rows_ref, place_ref, replicas, table_refs, selected):
-    stored = table_refs[0].shape[0]
+def collect(rows_ref, stored, arrived_ref, selected):
     batches = selected.shape[0]
-    me = place_ref[0]
-    for d in range(replicas):
-        owner = lax.rem(me + (replicas - d), replicas)
-        source = table_refs[d]
+    for owner in range(arrived_ref.shape[0]):
 
         def step(b, count):
             row = rows_ref[b] - owner * stored
@@ -227,7 +221,7 @@
 
             @pl.when(there)
             def _():
-                selected[b] = source[row if d == 0 else count]
+                selected[b] = arrived_ref[owner, count]
 
             return count + there.astype(jnp.int32)
 
@@ -250,15 +244,13 @@
     return lax.rem(row, forks) // batch_forks == column // rank
 
 
-def low_rank(attended, forks, own_rows, place, tables):
-    replicas = len(tables)
+def low_rank(attended, forks, own_rows, stored, arrived):
     rows, depth = attended.shape
     batches = own_rows.shape[0]
-    rank = tables[0].shape[1]
-
-    def kernel(rows_ref, place_ref, a_ref, *rest):
-        o_ref, selected = rest[-2], rest[-1]
-        collect(rows_ref, place_ref, replicas, rest[:replicas], selected)
+    rank = arrived.shape[2]
+
+    def kernel(rows_ref, a_ref, arrived_ref, o_ref, selected):
+        collect(rows_ref, stored, arrived_ref, selected)
         every = lax.dot_general(
             a_ref[...],
             selected[...].reshape(batches * rank, depth),
@@ -275,29 +267,25 @@
         kernel,
         out_shape=jax.ShapeDtypeStruct((rows, HD), F32),
         grid=(1,),
-        in_specs=[SMEM, SMEM, whole(attended.shape), whole(tables[0].shape)]
-        + [columns(t, depth, (t.shape[2] - depth) // depth) for t in tables[1:]],
+        in_specs=[SMEM, whole(attended.shape), columns(arrived, depth, (arrived.shape[3] - depth) // depth)],
         out_specs=whole((rows, HD)),
         scratch_shapes=[pltpu.VMEM((batches, rank, depth), BF16)],
         compiler_params=PARAMS,
         name="low_rank",
-    )(own_rows, place, attended, *tables)
-
-
-def finish(base, received, ranks, forks, own_rows, place, tables):
-    replicas = len(tables)
+    )(own_rows, attended, arrived)
+
+
+def finish(base, received, ranks, forks, own_rows, stored, arrived):
     rows, width = base.shape
     batches = own_rows.shape[0]
-    rank = tables[0].shape[1]
-    n_received, n_ranks = len(received), len(ranks)
-    steps = rows // forks
-
-    def kernel(rows_ref, place_ref, base_ref, *rest):
-        received_refs = rest[:n_received]
-        rank_refs = rest[n_received : n_received + n_ranks]
-        table_refs = rest[n_received + n_ranks : -2]
-        o_ref, selected = rest[-2], rest[-1]
-        collect(rows_ref, place_ref, replicas, table_refs, selected)
+    rank = arrived.shape[2]
+    n_received = len(received)
+    tile = min(width, 1024)
+
+    def kernel(rows_ref, base_ref, *rest):
+        received_refs, rank_refs = rest[:n_received], rest[n_received:-3]
+        arrived_ref, o_ref, selected = rest[-3:]
+        collect(rows_ref, stored, arrived_ref, selected)
         total = rank_refs[0][...]
         for r in rank_refs[1:]:
             total = total + r[...]
@@ -305,29 +293,28 @@
         spread = jnp.where(batch_mask(rows, forks, batches, rank), spread, 0.0)
         high = spread.astype(BF16)
         low = (spread - high.astype(F32)).astype(BF16)
-        up = selected[...].reshape(batches * rank, width)
-        tile = 512
-        for c in range(width // tile):
-            at = slice(c * tile, (c + 1) * tile)
-            out = jnp.dot(high, up[:, at], preferred_element_type=F32)
-            out = out + jnp.dot(low, up[:, at], preferred_element_type=F32)
-            out = out + base_ref[:, at]
-            for r in received_refs:
-                out = out + r[:, at].astype(F32)
-            o_ref[:, at] = out.astype(BF16)
-
+        up = selected[...].reshape(batches * rank, tile)
+        out = jnp.dot(high, up, preferred_element_type=F32)
+        out = out + jnp.dot(low, up, preferred_element_type=F32)
+        out = out + base_ref[...]
+        for r in received_refs:
+            out = out + r[...].astype(F32)
+        o_ref[...] = out.astype(BF16)
+
+    by_tile = pl.BlockSpec((rows, tile), lambda i: (0, i))
     return pl.pallas_call(
         kernel,
         out_shape=jax.ShapeDtypeStruct((rows, width), BF16),
-        grid=(1,),
-        in_specs=[SMEM, SMEM]
-        + [whole(x.shape) for x in (base, *received, *ranks, tables[0])]
-        + [columns(t, width, 0) for t in tables[1:]],
-        out_specs=whole((rows, width)),
-        scratch_shapes=[pltpu.VMEM((batches, rank, width), BF16)],
+        grid=(width // tile,),
+        in_specs=[SMEM, by_tile]
+        + [by_tile] * n_received
+        + [whole(r.shape) for r in ranks]
+        + [pl.BlockSpec(arrived.shape[:3] + (tile,), lambda i: (0, 0, 0, i))],
+        out_specs=by_tile,
+        scratch_shapes=[pltpu.VMEM((batches, rank, tile), BF16)],
         compiler_params=PARAMS,
         name="finish",
-    )(own_rows, place, base, *received, *ranks, *tables)
+    )(own_rows, base, *received, *ranks, arrived)
 
 
 def lookup(wanted, adapter_table_row):
@@ -362,11 +349,8 @@
     own_rows = lookup(batch_adapter_index, adapter_table_row)
     rows_all = lax.all_gather(own_rows, "replica")
     parts = pack(down_weight_table, up_weight_table, rows_all, place, capacity)
-    queries = lax.optimization_barrier((queries, *parts))[0]
-    arrived = [
-        lax.ppermute(parts[d - 1], "replica", [(z, (z + d) % replicas) for z in range(replicas)])
-        for d in range(1, replicas)
-    ]
+    queries = lax.optimization_barrier((queries, parts))[0]
+    arrived = lax.all_to_all(parts, "replica", 0, 0)
 
     lens = jnp.concatenate([prefix_length_each] * steps)[:, None]
     attended = attention(
@@ -396,10 +380,10 @@
         else:
             base = project(attended, output_weight, g + core, width, half, F32)
 
-    rank_part = low_rank(attended, forks, own_rows, place, [down_weight_table] + arrived)
+    rank_part = low_rank(attended, forks, own_rows, down_weight_table.shape[0], arrived)
     rank_chip = rank_part + lax.ppermute(rank_part, "tensor", swap)
     ranks = [rank_chip] + [lax.ppermute(rank_chip, "tensor", along(e)) for e in range(1, chips)]
-    out = finish(base, received, ranks, forks, own_rows, place, [up_weight_table] + arrived)
+    out = finish(base, received, ranks, forks, own_rows, up_weight_table.shape[0], arrived)
     return out.reshape(steps, forks, width).transpose(1, 0, 2)
 
 

time: 136 us -> 114 us (0.84)
  the two profiles are of different devices: /device:TPU:13 before, /device:TPU:0 now
where the time goes in v3:
time: 114 us; the launch traced here: 113 us
  Pallas kernels  46.1 us (40%)
  waiting for transfers between devices  36.3 us (32%)
  local copies, waits for them, and re-layouts  11.2 us (10%)
  blocking collectives  9.89 us (9%)
  starting transfers between devices  7.38 us (6%)
  other arithmetic  1.78 us (2%)
    all_to_all x1, waiting for transfers between devices, body(): arrived = lax.all_to_all(parts, 'replica', 0, 0)  34.8 us
    pallas_call x1, Pallas kernels, attention(): pl.pallas_call(functools.partial(attention_kernel, unit_heads, key_block)...  16.6 us
    pallas_call x4, Pallas kernels, project(): pl.pallas_call(kernel, out_shape=jax.ShapeDtypeStruct((rows, width), dtyp...  16.4 us
    unnamed x1, blocking collectives  9.89 us
    pallas_call x1, Pallas kernels, finish(): pl.pallas_call(kernel, out_shape=jax.ShapeDtypeStruct((rows, width), BF16...  5.68 us
    pallas_call x1, Pallas kernels, pack(): pl.pallas_call(kernel, out_shape=jax.ShapeDtypeStruct((replicas, capacity...  4.15 us
    all_to_all x1, starting transfers between devices, body(): arrived = lax.all_to_all(parts, 'replica', 0, 0)  3.84 us
    unnamed x17, local copies, waits for them, and re-layouts  3.78 us
  transfers between devices with their start and end apart: 6, of which 2 were waited for; matrix products, arithmetic and copies ran while one was open for 4% of the time, Pallas kernels for 32%

profile of v3, /device:TPU:0, one launch (start us, length us, event | category | flops | bytes accessed | tf_op | source)
XLA Modules:
  0.0 113.5 jit_solution(10487000891771743475)
XLA Ops:
  0.0 1.2 %dynamic-slice = u32[1]{0:T(128)} dynamic-slice(u32[32]{0:T(128)} %constant.31, u32[]{:T(128)S(6)} %add.25), dynamic_slice_sizes={1} | dynamic-slice | bytes 12
  1.9 0.9 select_reduce_fusion.rows_ref
  2.7 0.0 copy-start.5
  2.8 0.2 dynamic-update-slice
  3.0 9.9 %all-reduce = s32[64]{0:T(128)S(1)} all-reduce(s32[64]{0:T(128)S(1)} %dynamic-update-slice), channel_id=2, replica_groups=mesh['groups'=2,'replica'=4,'tensor'=4] {'replica'}, use_global_device_ids=true, to_apply=%add | all-reduce | flops 64 | bytes 512
  12.9 0.7 reshape.25.rows_ref
  13.6 4.2 %pack.1 = bf16[4,8,16,3072]{3,2,1,0:T(8,128)(2,1)} custom-call(s32[4,16]{1,0:T(4,128)} %reshape.25.rows_ref, s32[1]{0:T(128)} %bitcast.2.place_ref, bf16[16,16,1024]{2,1,0:T(8,128)(2,1)} %down_ref.1, bf16[16,16,2048]{2,1,0:T(8,128)(2,1)} %up_ref.1), custom_call_target="tpu_custom_call" | custom-call | tf_op jit(solution)/shard_map/pack/pallas_call | solution.py:204
  17.7 0.0 copy-start.6
  17.7 0.0 copy-start.3
  17.7 0.0 copy-start.4
  17.7 0.0 copy-done.5
  17.7 3.8 %all-to-all-start = ((bf16[4,8,16,3072]{3,2,1,0:T(8,128)(2,1)}), bf16[4,8,16,3072]{3,2,1,0:T(8,128)(2,1)S(1)}, u32[]{:S(2)}, u32[]{:S(2)}) async-start(bf16[4,8,16,3072]{3,2,1,0:T(8,128)(2,1)} %pack.1), calls=%async_computation | async-start | bytes 6291456 | tf_op jit(solution)/shard_map/all_to_all | solution.py:353
  21.6 0.0 copy-done.6
  21.6 0.8 copy.23.lens_ref
  22.4 2.0 %copy.30 = bf16[128,2,1024]{2,0,1:T(8,128)(2,1)} copy(bf16[128,2,1024]{2,1,0:T(2,128)(2,1)} %param.10) | data formatting | bytes 1048576 | tf_op jit(solution)/shard_map/optimization_barrier | solution.py:352
  24.4 0.0 copy-done.3
  24.4 0.0 copy-done.4
  24.4 0.7 copy_bitcast_fusion.2
  25.1 16.6 %attention.1.a_ref = bf16[256,1024]{1,0:T(8,128)(2,1)} custom-call(bf16[2,128,1024]{2,1,0:T(8,128)(2,1)} %bitcast.19, bf16[2,128,256]{2,1,0:T(8,128)(2,1)} %get-tuple-element.8.rk_ref, bf16[2,128,256]{2,1,0:T(8,128)(2,1)} %get-tuple-element.7.rv_ref, bf16[1,2,4096,256]{3,2,1,0:T(8,128)(2,1)} %kv_ref.1, s32[256,1]{1,0:T(8,128)} %copy.23.lens_ref), custom_call_target="tpu_custom_call" | custom-call | flops 20000000000 | bytes 6291456 | tf_op jit(solution)/shard_map/attention/pallas_call | solution.py:126
  41.6 4.0 %project.6 = bf16[256,2048]{1,0:T(8,128)(2,1)} custom-call(s32[1]{0:T(128)} %bitcast.9.group_ref, bf16[256,1024]{1,0:T(8,128)(2,1)} %attention.1.a_ref, bf16[1024,8192]{1,0:T(8,128)(2,1)} %w_ref.7), custom_call_target="tpu_custom_call" | custom-call | flops 1073741824 | bytes 4194304 | tf_op jit(solution)/shard_map/project/pallas_call | solution.py:165
  45.6 0.0 collective-permute-start.1
  45.6 3.9 %project.4 = bf16[256,2048]{1,0:T(8,128)(2,1)} custom-call(s32[1]{0:T(128)} %bitcast.7.group_ref, bf16[256,1024]{1,0:T(8,128)(2,1)} %attention.1.a_ref, bf16[1024,8192]{1,0:T(8,128)(2,1)} %w_ref.7), custom_call_target="tpu_custom_call" | custom-call | flops 1073741824 | bytes 4194304 | tf_op jit(solution)/shard_map/project/pallas_call | solution.py:165
  49.5 0.5 collective-permute-start
  50.0 0.0 collective-permute-done.1.rest_0_
  50.0 4.2 %project.7 = bf16[256,2048]{1,0:T(8,128)(2,1)} custom-call(s32[1]{0:T(128)} %bitcast.8.group_ref, bf16[256,1024]{1,0:T(8,128)(2,1)} %attention.1.a_ref, bf16[1024,8192]{1,0:T(8,128)(2,1)} %w_ref.7, bf16[256,2048]{1,0:T(8,128)(2,1)} %collective-permute-done.1.rest_0_), custom_call_target="tpu_custom_call" | custom-call | flops 1073741824 | bytes 4194304 | tf_op jit(solution)/shard_map/project/pallas_call | solution.py:165
  54.2 1.5 %collective-permute-start.2 = (bf16[256,2048]{1,0:T(8,128)(2,1)}, bf16[256,2048]{1,0:T(8,128)(2,1)}, u32[]{:S(2)}, u32[]{:S(2)}) collective-permute-start(bf16[256,2048]{1,0:T(8,128)(2,1)} %project.7), channel_id=1, source_target_pairs={{0,2},{1,3},{2,0},{3,1},{4,6},{5,7},{6,4},{7,5},{8,10},{9,11},{10,... | collective-permute-start | bytes 3145736 | tf_op jit(solution)/shard_map/ppermute | solution.py:379
  55.7 34.8 %all-to-all-done.arrived_ref.rest_3_ = bf16[4,8,16,3072]{3,2,1,0:T(8,128)(2,1)S(1)} async-done(((bf16[4,8,16,3072]{3,2,1,0:T(8,128)(2,1)}), bf16[4,8,16,3072]{3,2,1,0:T(8,128)(2,1)S(1)}, u32[]{:S(2)}, u32[]{:S(2)}) %all-to-all-start) | async-done | bytes 3145760 | tf_op jit(solution)/shard_map/all_to_all | solution.py:353
  90.5 0.0 copy-start
  90.5 1.6 %copy-done = bf16[4,8,16,3072]{3,2,1,0:T(8,128)(2,1)} copy-done((bf16[4,8,16,3072]{3,2,1,0:T(8,128)(2,1)}, bf16[4,8,16,3072]{3,2,1,0:T(8,128)(2,1)S(1)}, u32[]{:S(2)}) %copy-start) | copy-done | bytes 3145752
  92.1 3.4 %low_rank.1 = f32[256,128]{1,0:T(8,128)} custom-call(s32[16]{0:T(128)} %copy-done.5, bf16[256,1024]{1,0:T(8,128)(2,1)} %attention.1.a_ref, bf16[4,8,16,3072]{3,2,1,0:T(8,128)(2,1)} %copy-done), custom_call_target="tpu_custom_call" | custom-call | tf_op jit(solution)/shard_map/low_rank/pallas_call | solution.py:266
  95.5 0.0 collective-permute-start.3
  95.5 1.6 %collective-permute-done.3 = f32[256,128]{1,0:T(8,128)S(1)} collective-permute-done((f32[256,128]{1,0:T(8,128)}, f32[256,128]{1,0:T(8,128)S(1)}, u32[]{:S(2)}, u32[]{:S(2)}) %collective-permute-start.3) | collective-permute-done | bytes 131104 | tf_op jit(solution)/shard_map/ppermute | solution.py:384
  97.0 0.9 add.24.rest_1_
  98.0 0.0 copy-start.1
  98.0 1.5 %collective-permute-start.4 = (f32[256,128]{1,0:T(8,128)S(1)}, f32[256,128]{1,0:T(8,128)S(1)}, u32[]{:S(2)}, u32[]{:S(2)}) collective-permute-start(f32[256,128]{1,0:T(8,128)S(1)} %add.24.rest_1_), channel_id=1, source_target_pairs={{0,2},{1,3},{2,0},{3,1},{4,6},{5,7},{6,4},{7,5},{8,10},{9,11},{10,... | collective-permute-start | bytes 393224 | tf_op jit(solution)/shard_map/ppermute | solution.py:385
  99.5 0.0 collective-permute-done.rest_0_
  99.5 4.3 %project.5.base_ref = f32[256,2048]{1,0:T(8,128)} custom-call(s32[1]{0:T(128)} %bitcast.group_ref, bf16[256,1024]{1,0:T(8,128)(2,1)} %attention.1.a_ref, bf16[1024,8192]{1,0:T(8,128)(2,1)} %w_ref.7, bf16[256,2048]{1,0:T(8,128)(2,1)} %collective-permute-done.rest_0_), custom_call_target="tpu_custom_call" | custom-call | flops 1073741824 | bytes 4194304 | tf_op jit(solution)/shard_map/project/pallas_call | solution.py:165
  103.8 0.0 copy-done.1
  103.8 0.0 collective-permute-done.2.rest_0_
  103.8 0.0 collective-permute-done.4.rest_2_
  103.9 0.0 copy-start.2
  103.9 0.6 copy-done.2
  104.5 5.7 %finish.1 = bf16[256,2048]{1,0:T(8,128)(2,1)} custom-call(s32[16]{0:T(128)} %copy-done.5, f32[256,2048]{1,0:T(8,128)} %project.5.base_ref, bf16[256,2048]{1,0:T(8,128)(2,1)} %collective-permute-done.2.rest_0_, f32[256,128]{1,0:T(8,128)} %copy-done.1, f32[256,128]{1,0:T(8,128)} %copy-done.2, bf16[4,8,16,3072]{3,2,1,0:T(8,128)(2,1)} %copy-done), custom_call_target="tpu_custom_call" | custom-call | tf_op jit(solution)/shard_map/finish/pallas_call | solution.py:305
  110.2 3.3 %copy.29 = bf16[2,128,2048]{2,0,1:T(2,128)(2,1)} copy(bf16[2,128,2048]{2,1,0:T(8,128)(2,1)} %bitcast.18) | data formatting | bytes 2097152 | tf_op jit(solution)/shard_map/reshape | solution.py:387
  (2 shorter events, 0.0 us)
Async XLA Ops:
  2.7 15.0 %copy-start.5 = (s32[16]{0:T(128)}, s32[16]{0:T(128)S(1)}, u32[]{:S(2)}) copy-start(s32[16]{0:T(128)S(1)} %select_reduce_fusion.rows_ref) | copy-start | bytes 196
  17.7 3.9 %copy-start.6 = (s32[128]{0:T(128)S(1)}, s32[128]{0:T(128)}, u32[]{:S(2)}) copy-start(s32[128]{0:T(128)} %param.14) | copy-start | bytes 1540
  17.7 6.6 %copy-start.3 = (bf16[128,2,256]{2,1,0:T(2,128)(2,1)S(1)}, bf16[128,2,256]{2,1,0:T(2,128)(2,1)}, u32[]{:S(2)}) copy-start(bf16[128,2,256]{2,1,0:T(2,128)(2,1)} %param.12) | copy-start | bytes 393220
  17.7 6.6 %copy-start.4 = (bf16[128,2,256]{2,1,0:T(2,128)(2,1)S(1)}, bf16[128,2,256]{2,1,0:T(2,128)(2,1)}, u32[]{:S(2)}) copy-start(bf16[128,2,256]{2,1,0:T(2,128)(2,1)} %param.11) | copy-start | bytes 393220
  17.7 72.7 %all-to-all-start = ((bf16[4,8,16,3072]{3,2,1,0:T(8,128)(2,1)}), bf16[4,8,16,3072]{3,2,1,0:T(8,128)(2,1)S(1)}, u32[]{:S(2)}, u32[]{:S(2)}) async-start(bf16[4,8,16,3072]{3,2,1,0:T(8,128)(2,1)} %pack.1), calls=%async_computation | async-start | bytes 6291456 | tf_op jit(solution)/shard_map/all_to_all | solution.py:353
  45.6 4.4 %collective-permute-start.1 = (bf16[256,2048]{1,0:T(8,128)(2,1)}, bf16[256,2048]{1,0:T(8,128)(2,1)}, u32[]{:S(2)}, u32[]{:S(2)}) collective-permute-start(bf16[256,2048]{1,0:T(8,128)(2,1)} %project.6), channel_id=1, source_target_pairs={{0,1},{1,0},{2,3},{3,2},{4,5},{5,4},{6,7},{7,6},{8,9},{9,8},{10,11... | collective-permute-start | bytes 3145736 | tf_op jit(solution)/shard_map/ppermute | solution.py:372
  49.5 50.0 %collective-permute-start = (bf16[256,2048]{1,0:T(8,128)(2,1)}, bf16[256,2048]{1,0:T(8,128)(2,1)}, u32[]{:S(2)}, u32[]{:S(2)}) collective-permute-start(bf16[256,2048]{1,0:T(8,128)(2,1)} %project.4), channel_id=1, source_target_pairs={{0,1},{1,0},{2,3},{3,2},{4,5},{5,4},{6,7},{7,6},{8,9},{9,8},{10,11... | collective-permute-start | bytes 3145736 | tf_op jit(solution)/shard_map/ppermute | solution.py:372
  54.2 49.6 %collective-permute-start.2 = (bf16[256,2048]{1,0:T(8,128)(2,1)}, bf16[256,2048]{1,0:T(8,128)(2,1)}, u32[]{:S(2)}, u32[]{:S(2)}) collective-permute-start(bf16[256,2048]{1,0:T(8,128)(2,1)} %project.7), channel_id=1, source_target_pairs={{0,2},{1,3},{2,0},{3,1},{4,6},{5,7},{6,4},{7,5},{8,10},{9,11},{10,... | collective-permute-start | bytes 3145736 | tf_op jit(solution)/shard_map/ppermute | solution.py:379
  90.5 1.6 %copy-start = (bf16[4,8,16,3072]{3,2,1,0:T(8,128)(2,1)}, bf16[4,8,16,3072]{3,2,1,0:T(8,128)(2,1)S(1)}, u32[]{:S(2)}) copy-start(bf16[4,8,16,3072]{3,2,1,0:T(8,128)(2,1)S(1)} %all-to-all-done.arrived_ref.rest_3_) | copy-start | bytes 9437188
  95.5 1.6 %collective-permute-start.3 = (f32[256,128]{1,0:T(8,128)}, f32[256,128]{1,0:T(8,128)S(1)}, u32[]{:S(2)}, u32[]{:S(2)}) collective-permute-start(f32[256,128]{1,0:T(8,128)} %low_rank.1), channel_id=1, source_target_pairs={{0,1},{1,0},{2,3},{3,2},{4,5},{5,4},{6,7},{7,6},{8,9},{9,8},{10,11... | collective-permute-start | bytes 393224 | tf_op jit(solution)/shard_map/ppermute | solution.py:384
  98.0 5.9 %copy-start.1 = (f32[256,128]{1,0:T(8,128)}, f32[256,128]{1,0:T(8,128)S(1)}, u32[]{:S(2)}) copy-start(f32[256,128]{1,0:T(8,128)S(1)} %add.24.rest_1_) | copy-start | bytes 393220
  98.0 5.9 %collective-permute-start.4 = (f32[256,128]{1,0:T(8,128)S(1)}, f32[256,128]{1,0:T(8,128)S(1)}, u32[]{:S(2)}, u32[]{:S(2)}) collective-permute-start(f32[256,128]{1,0:T(8,128)S(1)} %add.24.rest_1_), channel_id=1, source_target_pairs={{0,2},{1,3},{2,0},{3,1},{4,6},{5,7},{6,4},{7,5},{8,10},{9,11},{10,... | collective-permute-start | bytes 393224 | tf_op jit(solution)/shard_map/ppermute | solution.py:385
  103.9 0.7 copy-start.2
